TPU v7x, 128 devices: a whole 4x4x4 slice. The times are simulated.
128 devices in a mesh: dp: 16 (over z, y_lo, core), tensor: 8 (over y_hi, x).
Axes of the slice: x: 4, y: 4 (y_hi: 2, y_lo: 2; y = y_hi * 2 + y_lo), z: 4, core: 2. Of those that a mesh axis runs over, the one named last changes fastest.
Arguments:
- tokens: bfloat16 [16384, 2048], P(('dp', 'tensor')), may hold values from -6 to 6
- cotangent: bfloat16 [16384, 2048], P(('dp', 'tensor')), may hold values from -6 to 6
- doc_lengths: int32 [16, 4], P('dp'), may hold values from 1 to 1021, as said below
- query_weight: float32 [2048, 2048], P('dp', 'tensor'), may hold values from -0.125 to 0.125
- key_value_weight: float32 [2, 2048, 1024], P(None, 'dp', 'tensor'), may hold values from -0.125 to 0.125
- output_weight: float32 [2048, 2048], P('tensor', 'dp'), may hold values from -1.5 to 1.5
- gateup_weight: float32 [2, 2048, 6144], P(None, 'dp', 'tensor'), may hold values from -0.125 to 0.125
- down_weight: float32 [6144, 2048], P('tensor', 'dp'), may hold values from -0.078125 to 0.078125
- norm_gains: float32 [4352], P(('dp', 'tensor')), may hold values from 0.5 to 1.5
- query_momentum: float32 [2048, 2048], P('dp', 'tensor')
- keyval_momentum: float32 [2, 2048, 1024], P(None, 'dp', 'tensor')
- output_momentum: float32 [2048, 2048], P('tensor', 'dp')
- gateup_momentum: float32 [2, 2048, 6144], P(None, 'dp', 'tensor')
- down_momentum: float32 [6144, 2048], P('tensor', 'dp')
- gains_momentum: float32 [4352], P(('dp', 'tensor'))
- query_average: float32 [2048, 2048], P('dp', 'tensor'), may hold values from -0.125 to 0.125
- key_value_mean: float32 [2, 2048, 1024], P(None, 'dp', 'tensor'), may hold values from -0.125 to 0.125
- output_average: float32 [2048, 2048], P('tensor', 'dp'), may hold values from -1.5 to 1.5
- gateup_average: float32 [2, 2048, 6144], P(None, 'dp', 'tensor'), may hold values from -0.125 to 0.125
- down_average: float32 [6144, 2048], P('tensor', 'dp'), may hold values from -0.078125 to 0.078125
- gains_average: float32 [4352], P(('dp', 'tensor')), may hold values from 0.2 to 1.8
Outputs:
- block_out: bfloat16 [16384, 2048], P(('dp', 'tensor'))
- input_grad: bfloat16 [16384, 2048], P(('dp', 'tensor'))
- query_updated: float32 [2048, 2048], P('dp', 'tensor')
- keyval_updated: float32 [2, 2048, 1024], P(None, 'dp', 'tensor')
- output_updated: float32 [2048, 2048], P('tensor', 'dp')
- gateup_updated: float32 [2, 2048, 6144], P(None, 'dp', 'tensor')
- down_updated: float32 [6144, 2048], P('tensor', 'dp')
- gains_updated: float32 [4352], P(('dp', 'tensor'))
- query_velocity: float32 [2048, 2048], P('dp', 'tensor')
- keyval_velocity: float32 [2, 2048, 1024], P(None, 'dp', 'tensor')
- output_velocity: float32 [2048, 2048], P('tensor', 'dp')
- gateup_velocity: float32 [2, 2048, 6144], P(None, 'dp', 'tensor')
- down_velocity: float32 [6144, 2048], P('tensor', 'dp')
- gains_velocity: float32 [4352], P(('dp', 'tensor'))
- query_smoothed: float32 [2048, 2048], P('dp', 'tensor')
- keyval_smoothed: float32 [2, 2048, 1024], P(None, 'dp', 'tensor')
- output_smoothed: float32 [2048, 2048], P('tensor', 'dp')
- gateup_smoothed: float32 [2, 2048, 6144], P(None, 'dp', 'tensor')
- down_smoothed: float32 [6144, 2048], P('tensor', 'dp')
- gains_smoothed: float32 [4352], P(('dp', 'tensor'))
Inputs may be any that keep to these rules, and one draw needn't show every extreme that they name: `doc_lengths`: row g holds the lengths of group g's 4 documents in order, summing to 1024; the first, third and fourth are each at least 1 and under 1024 // 8, the third and fourth together under 1024 // 8.
All inputs are finite; a program needn't handle non-finite values.
Results may differ from a plain program's by a relative error of at most 0.02.
Values may be sent and summed in bfloat16 or wider, within the bound.
A program may use at most 192 MiB of HBM per device.

v0:
```python
import math

import jax
import jax.numpy as jnp
from jax import lax
from jax.sharding import PartitionSpec as P

MODEL_WIDTH = 2048
QUERY_HEADS = 16
HEAD_SIZE = 128
FF = 6144


EPSILON = 1e-06
MOMENTUM = 0.9
AVERAGING = 0.5
ROPE_BASE = 1000000.0


def gather_turned(arrays, axis, dims):
    turned = [jnp.moveaxis(a, dim, 0) for a, dim in zip(arrays, dims)]
    widths = [t[0].size for t in turned]
    both = jnp.concatenate([t.reshape(-1, w) for t, w in zip(turned, widths)], axis=1)
    whole = lax.all_gather(both, axis, axis=0, tiled=True)
    tiles = jnp.split(whole, [sum(widths[:k]) for k in range(1, len(widths))], axis=1)
    return tuple(
        (
            jnp.moveaxis(b.reshape(-1, *t.shape[1:]), 0, dim)
            for b, t, dim in zip(tiles, turned, dims)
        )
    )


def cut_along(shard, dim, length):
    dims = shard.shape
    tiles = shard.reshape(*dims[:dim], length, dims[dim] // length, *dims[dim + 1 :])
    return jnp.moveaxis(tiles, dim, 0)


def summed_on_arrival(shard, axis, dim):
    tiles = cut_along(shard, dim, lax.axis_size(axis))
    arrived = lax.all_to_all(tiles, axis, split_axis=0, concat_axis=0, tiled=True)
    return arrived.astype(jnp.float32).sum(axis=0)


def root_mean_norm(value_vectors, scaling):
    return (
        value_vectors
        * lax.rsqrt(jnp.mean(value_vectors * value_vectors, axis=-1, keepdims=True) + EPSILON)
        * scaling
    )


def rotary_embed(value_vectors, cosine_table, sine_table):
    middle = value_vectors.shape[-1] // 2
    turned = jnp.concatenate([-value_vectors[..., middle:], value_vectors[..., :middle]], axis=-1)
    return value_vectors * cosine_table + turned * sine_table


def doc_layout(length_row, row_total_count):
    doc_ends = jnp.cumsum(length_row)
    places = jnp.arange(row_total_count, dtype=jnp.int32)
    passed = places[:, None] >= doc_ends[None, :]
    segment = jnp.sum(passed.astype(jnp.int32), axis=1)
    starts = jnp.sum(jnp.where(passed, length_row[None, :], 0), axis=1)
    position = places - starts
    halves = jnp.arange(HEAD_SIZE // 2, dtype=jnp.float32)
    inverse = ROPE_BASE ** (-2.0 * halves / HEAD_SIZE)
    angles = position.astype(jnp.float32)[:, None] * inverse[None, :]
    angles = jnp.concatenate([angles, angles], axis=-1)
    return (segment, places, jnp.cos(angles), jnp.sin(angles))


def step_rates(total_tokens):
    root_tokens = math.sqrt(total_tokens)
    narrow = MODEL_WIDTH ** (-0.5)
    return (
        narrow / (2.0 * root_tokens),
        narrow / (2.0 * root_tokens),
        (QUERY_HEADS * HEAD_SIZE // 128) ** (-0.5) / (0.24 * root_tokens),
        narrow / (0.7 * root_tokens),
        FF ** (-0.5) / (1.2 * root_tokens),
        0.025 / root_tokens,
    )


def swiglu(gate_value, upward):
    return jax.nn.silu(gate_value) * upward


def head_turn(projected, scaling, cosine_table, sine_table):
    heads = projected.reshape(projected.shape[0], -1, HEAD_SIZE)
    return rotary_embed(
        root_mean_norm(heads, scaling), cosine_table[:, None, :], sine_table[:, None, :]
    )


def product(left, right):
    return jnp.dot(left, right, preferred_element_type=jnp.float32)


def contract_last(left, right):
    return lax.dot_general(
        left, right, (((1,), (1,)), ((), ())), preferred_element_type=jnp.float32
    )


def contract_first(left, right):
    return lax.dot_general(
        left, right, (((0,), (0,)), ((), ())), preferred_element_type=jnp.float32
    )


def scores_for(query_tile_block, key_vectors):
    return jnp.einsum(
        "qkgd,skd->kgqs", query_tile_block, key_vectors, preferred_element_type=jnp.float32
    ) * HEAD_SIZE ** (-0.5)


def mask_for(segment_block, place_block, segment, places):
    return (segment_block[:, None] == segment[None, :]) & (places[None, :] <= place_block[:, None])


def attend_forward(queries, key_vectors, value_vectors, segment, places, block_row_span):
    row_total_count = queries.shape[0]
    key_heads = key_vectors.shape[1]
    sharing = queries.shape[1] // key_heads
    blocks = row_total_count // block_row_span
    grouped_heads = queries.reshape(blocks, block_row_span, key_heads, sharing, HEAD_SIZE)

    def one_block(element):
        query_tile_block, segment_block, place_block = element
        allowed = mask_for(segment_block, place_block, segment, places)
        scores = jnp.where(allowed, scores_for(query_tile_block, key_vectors), -1e30)
        highest = jnp.max(scores, axis=-1, keepdims=True)
        weights = jnp.exp(scores - highest)
        summed = jnp.sum(weights, axis=-1, keepdims=True)
        probability = (weights / summed).astype(jnp.bfloat16)
        blended = jnp.einsum(
            "kgqs,skd->qkgd", probability, value_vectors, preferred_element_type=jnp.float32
        )
        return (blended.reshape(block_row_span, -1), highest + jnp.log(summed))

    return lax.map(
        one_block,
        (
            grouped_heads,
            segment.reshape(blocks, block_row_span),
            places.reshape(blocks, block_row_span),
        ),
    )


def attend_backward(
    queries, key_vectors, value_vectors, out_grad, log_totals, segment, places, block_row_span
):
    row_total_count = queries.shape[0]
    key_heads = key_vectors.shape[1]
    sharing = queries.shape[1] // key_heads
    blocks = row_total_count // block_row_span
    scaling = HEAD_SIZE ** (-0.5)
    grouped_heads = queries.reshape(blocks, block_row_span, key_heads, sharing, HEAD_SIZE)
    grad_grouped = out_grad.reshape(blocks, block_row_span, key_heads, sharing, HEAD_SIZE)

    def one_block(running, element):
        key_sum, value_sum = running
        query_tile_block, grad_block, log_block, segment_block, place_block = element
        allowed = mask_for(segment_block, place_block, segment, places)
        scores = scores_for(query_tile_block, key_vectors)
        probability = jnp.where(allowed, jnp.exp(scores - log_block), 0.0)
        probability_low = probability.astype(jnp.bfloat16)
        value_sum = value_sum + jnp.einsum(
            "kgqs,qkgd->skd", probability_low, grad_block, preferred_element_type=jnp.float32
        )
        prob_grad = jnp.einsum(
            "qkgd,skd->kgqs", grad_block, value_vectors, preferred_element_type=jnp.float32
        )
        centre = jnp.sum(probability * prob_grad, axis=-1, keepdims=True)
        score_grad = (probability * (prob_grad - centre)).astype(jnp.bfloat16)
        query_grad = (
            jnp.einsum(
                "kgqs,skd->qkgd", score_grad, key_vectors, preferred_element_type=jnp.float32
            )
            * scaling
        )
        key_sum = (
            key_sum
            + jnp.einsum(
                "kgqs,qkgd->skd", score_grad, query_tile_block, preferred_element_type=jnp.float32
            )
            * scaling
        )
        return ((key_sum, value_sum), query_grad.reshape(block_row_span, -1, HEAD_SIZE))

    empty = jnp.zeros(key_vectors.shape, jnp.float32)
    (key_grad, value_grad), query_grads = lax.scan(
        one_block,
        (empty, empty),
        (
            grouped_heads,
            grad_grouped,
            log_totals,
            segment.reshape(blocks, block_row_span),
            places.reshape(blocks, block_row_span),
        ),
    )
    return (query_grads.reshape(row_total_count, -1, HEAD_SIZE), key_grad, value_grad)


def body(
    tokens,
    cotangent,
    doc_lengths,
    query_weight,
    key_value_weight,
    output_weight,
    gateup_weight,
    down_weight,
    norm_gains,
    query_momentum,
    keyval_momentum,
    output_momentum,
    gateup_momentum,
    down_momentum,
    gains_momentum,
    query_average,
    key_value_mean,
    output_average,
    gateup_average,
    down_average,
    gains_average,
):
    tensor_count = lax.axis_size("tensor")
    data_count = lax.axis_size("dp")
    own_rows = tokens.shape[0]
    group_rows = own_rows * tensor_count
    block_row_span = min(512, group_rows)
    rates = step_rates(group_rows * data_count)
    lowered = (
        query_weight.astype(jnp.bfloat16),
        key_value_weight.astype(jnp.bfloat16),
        output_weight.astype(jnp.bfloat16),
        gateup_weight.astype(jnp.bfloat16),
        down_weight.astype(jnp.bfloat16),
    )
    gathered = gather_turned(
        (lowered[0], lowered[1], lowered[2], lowered[3], lowered[4]), "dp", (0, 1, 1, 1, 1)
    )
    query_full, keyval_full, output_full, gateup_full, down_full = gathered
    gains_full = lax.all_gather(norm_gains, ("dp", "tensor"), axis=0, tiled=True)
    gain_first = gains_full[:MODEL_WIDTH]
    gain_second = gains_full[MODEL_WIDTH : 2 * MODEL_WIDTH]
    gain_query = gains_full[2 * MODEL_WIDTH : 2 * MODEL_WIDTH + HEAD_SIZE]
    key_norm_gain = gains_full[2 * MODEL_WIDTH + HEAD_SIZE :]
    segment, places, cosine_table, sine_table = doc_layout(doc_lengths[0], group_rows)
    inputs = tokens.astype(jnp.float32)
    first_normed, first_pull = jax.vjp(root_mean_norm, inputs, gain_first)
    first_low = first_normed.astype(jnp.bfloat16)
    portion = lax.all_gather(first_low, "tensor", axis=0, tiled=True)
    normed_all = portion
    query_part = product(portion, query_full)
    key_slice = product(portion, keyval_full[0])
    value_slice = product(portion, keyval_full[1])

    def turn_both(query_in, key_in, query_scale, key_scale):
        return (
            head_turn(query_in, query_scale, cosine_table, sine_table),
            head_turn(key_in, key_scale, cosine_table, sine_table),
        )

    (query_turned, key_turned), turn_pull = jax.vjp(
        turn_both, query_part, key_slice, gain_query, key_norm_gain
    )
    queries = query_turned.astype(jnp.bfloat16)
    key_vectors = key_turned.astype(jnp.bfloat16)
    value_vectors = value_slice.astype(jnp.bfloat16).reshape(group_rows, -1, HEAD_SIZE)
    attended, log_totals = attend_forward(
        queries, key_vectors, value_vectors, segment, places, block_row_span
    )
    attended_low = attended.reshape(group_rows, -1).astype(jnp.bfloat16)
    attention_out = lax.psum_scatter(
        product(attended_low, output_full).astype(jnp.bfloat16),
        "tensor",
        scatter_dimension=0,
        tiled=True,
    ).astype(jnp.float32)
    residual = inputs + attention_out
    second_normed, second_pull = jax.vjp(root_mean_norm, residual, gain_second)
    second_low = second_normed.astype(jnp.bfloat16)
    portion = lax.all_gather(second_low, "tensor", axis=0, tiled=True)
    gate_value = product(portion, gateup_full[0])
    upward = product(portion, gateup_full[1])
    activated, swiglu_pull = jax.vjp(swiglu, gate_value, upward)
    hidden = activated.astype(jnp.bfloat16)
    mlp_out = lax.psum_scatter(
        product(hidden, down_full).astype(jnp.bfloat16), "tensor", scatter_dimension=0, tiled=True
    ).astype(jnp.float32)
    block_out = (residual + mlp_out).astype(jnp.bfloat16)
    query_back, keyval_back, output_back, gateup_back, down_back = gathered
    upstream_all = lax.all_gather(cotangent, "tensor", axis=0, tiled=True)
    hidden_grad = contract_last(upstream_all, down_back)
    down_grad = contract_first(hidden, upstream_all)
    gate_grad, upward_grad = swiglu_pull(hidden_grad)
    gate_low = gate_grad.astype(jnp.bfloat16)
    upward_low = upward_grad.astype(jnp.bfloat16)
    gateup_grad = jnp.stack(
        [contract_first(portion, gate_low), contract_first(portion, upward_low)]
    )
    gateup_total, down_total = (
        lax.psum_scatter(
            gateup_grad.astype(jnp.bfloat16), "dp", scatter_dimension=1, tiled=True
        ).astype(jnp.float32),
        lax.psum_scatter(
            down_grad.astype(jnp.bfloat16), "dp", scatter_dimension=1, tiled=True
        ).astype(jnp.float32),
    )
    second_grad = lax.psum_scatter(
        (
            contract_last(gate_low, gateup_back[0]) + contract_last(upward_low, gateup_back[1])
        ).astype(jnp.bfloat16),
        "tensor",
        scatter_dimension=0,
        tiled=True,
    ).astype(jnp.float32)
    residual_part, second_gain_grad = second_pull(second_grad)
    residual_grad = cotangent.astype(jnp.float32) + residual_part
    residual_low = residual_grad.astype(jnp.bfloat16)
    residual_all = lax.all_gather(residual_low, "tensor", axis=0, tiled=True)
    output_grad = contract_first(attended_low, residual_all)
    attended_grad = contract_last(residual_all, output_back).astype(jnp.bfloat16)
    query_rot_grad, key_rot_grad, value_grad = attend_backward(
        queries,
        key_vectors,
        value_vectors,
        attended_grad,
        log_totals,
        segment,
        places,
        block_row_span,
    )
    query_part_grad, key_part_grad, query_gain_grad, key_gain_grad = turn_pull(
        (query_rot_grad, key_rot_grad)
    )
    query_low = query_part_grad.astype(jnp.bfloat16)
    key_low = key_part_grad.astype(jnp.bfloat16)
    value_low = value_grad.reshape(group_rows, -1).astype(jnp.bfloat16)
    query_grad = contract_first(normed_all, query_low)
    keyval_grad = jnp.stack(
        [contract_first(normed_all, key_low), contract_first(normed_all, value_low)]
    )
    first_grad = lax.psum_scatter(
        (
            contract_last(query_low, query_back)
            + contract_last(key_low, keyval_back[0])
            + contract_last(value_low, keyval_back[1])
        ).astype(jnp.bfloat16),
        "tensor",
        scatter_dimension=0,
        tiled=True,
    ).astype(jnp.float32)
    input_part, first_gain_grad = first_pull(first_grad)
    input_grad = (residual_grad + input_part).astype(jnp.bfloat16)
    gain_terms = jnp.concatenate(
        [first_gain_grad, second_gain_grad, query_gain_grad, key_gain_grad]
    )
    query_total, keyval_total, output_total = (
        summed_on_arrival(query_grad.astype(jnp.bfloat16), "dp", 0),
        summed_on_arrival(keyval_grad.astype(jnp.bfloat16), "dp", 1),
        summed_on_arrival(output_grad.astype(jnp.bfloat16), "dp", 1),
    )
    gains_total = lax.psum_scatter(gain_terms, ("dp", "tensor"), scatter_dimension=0, tiled=True)
    masters = (
        query_weight,
        key_value_weight,
        output_weight,
        gateup_weight,
        down_weight,
        norm_gains,
    )
    gradients = (query_total, keyval_total, output_total, gateup_total, down_total, gains_total)
    moments = (
        query_momentum,
        keyval_momentum,
        output_momentum,
        gateup_momentum,
        down_momentum,
        gains_momentum,
    )
    averages = (
        query_average,
        key_value_mean,
        output_average,
        gateup_average,
        down_average,
        gains_average,
    )
    updated = []
    velocity = []
    smoothed = []
    for master, gradient, moment, average, rate in zip(
        masters, gradients, moments, averages, rates
    ):
        moment_next = MOMENTUM * moment + gradient
        master_next = master - rate * (gradient + MOMENTUM * moment_next)
        updated.append(master_next)
        velocity.append(moment_next)
        smoothed.append(AVERAGING * average + (1.0 - AVERAGING) * master_next)
    return (
        block_out,
        input_grad,
        updated[0],
        updated[1],
        updated[2],
        updated[3],
        updated[4],
        updated[5],
        velocity[0],
        velocity[1],
        velocity[2],
        velocity[3],
        velocity[4],
        velocity[5],
        smoothed[0],
        smoothed[1],
        smoothed[2],
        smoothed[3],
        smoothed[4],
        smoothed[5],
    )


def solution(mesh):
    return jax.shard_map(
        body,
        mesh=mesh,
        in_specs=(
            P(("dp", "tensor"), None),
            P(("dp", "tensor"), None),
            P("dp", None),
            P("dp", "tensor"),
            P(None, "dp", "tensor"),
            P("tensor", "dp"),
            P(None, "dp", "tensor"),
            P("tensor", "dp"),
            P(("dp", "tensor")),
            P("dp", "tensor"),
            P(None, "dp", "tensor"),
            P("tensor", "dp"),
            P(None, "dp", "tensor"),
            P("tensor", "dp"),
            P(("dp", "tensor")),
            P("dp", "tensor"),
            P(None, "dp", "tensor"),
            P("tensor", "dp"),
            P(None, "dp", "tensor"),
            P("tensor", "dp"),
            P(("dp", "tensor")),
        ),
        out_specs=(
            P(("dp", "tensor"), None),
            P(("dp", "tensor"), None),
            P("dp", "tensor"),
            P(None, "dp", "tensor"),
            P("tensor", "dp"),
            P(None, "dp", "tensor"),
            P("tensor", "dp"),
            P(("dp", "tensor")),
            P("dp", "tensor"),
            P(None, "dp", "tensor"),
            P("tensor", "dp"),
            P(None, "dp", "tensor"),
            P("tensor", "dp"),
            P(("dp", "tensor")),
            P("dp", "tensor"),
            P(None, "dp", "tensor"),
            P("tensor", "dp"),
            P(None, "dp", "tensor"),
            P("tensor", "dp"),
            P(("dp", "tensor")),
        ),
        check_vma=False,
    )
```

profile of v0, /device:TPU:1, one launch (start us, length us, event | category | flops | bytes accessed | tf_op | source)
XLA Modules:
  0.0 981.4 jit_solution(11323326016151256928)
XLA Ops:
  14.0 68.9 %all-reduce.4 = f32[4352]{0:T(1024)S(1)} all-reduce(f32[4352]{0:T(1024)S(1)} %dynamic-update-slice), channel_id=1, replica_groups=mesh['dp'=16,'tensor'=8] {'dp','tensor'}, use_global_device_ids=true, to_apply=%add.4 | all-reduce | flops 4352 | bytes 34816
  85.6 9.1 fusion.112
  100.2 71.3 %all-gather.6.cloned.1.call-done = bf16[1024,2048]{1,0:T(8,128)(2,1)} async-done(((bf16[128,2048]{1,0:T(8,128)(2,1)}), bf16[1024,2048]{1,0:T(8,128)(2,1)}) %all-gather.6.cloned.1.call-update) | async-done | bytes 4194320 | tf_op jit(solution)/shard_map/all_gather | solution.py:259
  198.1 11.7 %while.28 = (s32[]{:T(128)}, bf16[2,512,256]{2,1,0:T(8,128)(2,1)}, f32[2,1,2,512,1]{3,2,4,1,0:T(2,128)S(1)}, s32[2,512]{1,0:T(2,128)S(1)}, s32[1024]{0:T(1024)S(...) while((s32[]{:T(128)}, bf16[2,512,256]{2,1,0:T(8,128)(2,1)}, ...), condition=%wide.region_9.10_spmd.clone, body=%wide.region_6.9_spmd.clone.sunk | while | flops 551025664 | bytes 22069456 | solution.py:144
  209.8 4.6 convolution_convert_fusion
  214.5 82.0 %reduce-scatter.9.cloned.1.call-done = bf16[128,2048]{1,0:T(8,128)(2,1)} async-done(((bf16[1024,2048]{1,0:T(8,128)(2,1)}), bf16[128,2048]{1,0:T(8,128)(2,1)}) %reduce-scatter.9.cloned.1.call-update) | async-done | bytes 524304 | tf_op jit(solution)/shard_map/reduce_scatter | solution.py:281
  300.5 6.6 split.39
  307.1 8.9 copy.180
  316.0 55.2 %all-gather.10.cloned.1.call-done = bf16[1024,2048]{1,0:T(8,128)(2,1)} async-done(((bf16[128,2048]{1,0:T(8,128)(2,1)}), bf16[1024,2048]{1,0:T(8,128)(2,1)}) %all-gather.10.cloned.1.call-update) | async-done | bytes 4194320 | tf_op jit(solution)/shard_map/all_gather | solution.py:290
  371.2 8.4 fusion.62
  379.6 5.1 fusion.61
  384.8 58.1 %all-gather.12.cloned.1.call-done = bf16[1024,2048]{1,0:T(8,128)(2,1)} async-done(((bf16[128,2048]{1,0:T(8,128)(2,1)}), bf16[1024,2048]{1,0:T(8,128)(2,1)}) %all-gather.12.cloned.1.call-update) | async-done | bytes 4194320 | tf_op jit(solution)/shard_map/all_gather | solution.py:300
  442.9 10.6 %fusion.56 = (bf16[1024,768]{1,0:T(8,128)(2,1)S(1)}, bf16[1024,768]{1,0:T(8,128)(2,1)S(1)}, bf16[1024,768]{1,0:T(8,128)(2,1)}) fusion(f32[1024,768]{1,0:T(8,128)} %fusion.61, f32[1024,768]{1,0:T(8,128)} %fusion.62, bf16[1024,2048]{1,0:T(8,128)(2,1)} %all-gather.12.cloned.1.call-done, bf16[2048,3072]{0,1:T(8,128)(2,1)} %all-gather.8.cloned.1.call-done), kind=kOutput, calls=%fused_computation.81 | convolution fusion | flops 3233808384 | bytes 18350080 | tf_op jit(solution)/shard_map/dot_general | solution.py:103
  453.4 6.5 fusion.60
  459.9 7.2 add_convert_fusion.1
  467.2 82.1 %reduce-scatter.13.cloned.1.call-done = bf16[128,2048]{1,0:T(8,128)(2,1)} async-done(((bf16[1024,2048]{1,0:T(8,128)(2,1)}), bf16[128,2048]{1,0:T(8,128)(2,1)}) %reduce-scatter.13.cloned.1.call-update) | async-done | bytes 524304 | tf_op jit(solution)/shard_map/reduce_scatter | solution.py:317
  553.7 7.8 convolution_convert_fusion.2
  561.5 4.7 copy.201
  566.3 6.4 fusion.59
  580.2 44.7 %all-gather.14.cloned.1.call-done = bf16[1024,2048]{1,0:T(8,128)(2,1)} async-done(((bf16[128,2048]{1,0:T(8,128)(2,1)}), bf16[1024,2048]{1,0:T(8,128)(2,1)}) %all-gather.14.cloned.1.call-update) | async-done | bytes 4194320 | tf_op jit(solution)/shard_map/all_gather | solution.py:328
  630.7 17.1 %while.29 = (s32[]{:T(128)}, f32[1024,1,128]{0,2,1:T(8,128)S(1)}, f32[1024,1,128]{0,2,1:T(8,128)}, f32[2,512,2,128]{3,1,0,2:T(8,128)}, bf16[2,512,1,2,128]{4,1,3...) while((s32[]{:T(128)}, f32[1024,1,128]{0,2,1:T(8,128)S(1)}, ...), condition=%wide.region_17.18_spmd.clone, body=%wide.region_15.17_spmd.clone.sunk | while | flops 1360264192 | bytes 51163420 | solution.py:196
  659.3 4.7 add_convert_fusion
  664.1 7.8 convolution_convert_fusion.1
  677.7 5.5 all-to-all-start.2
  687.8 13.2 %all-to-all-done.2 = bf16[16,256,128]{2,1,0:T(8,128)(2,1)S(1)} async-done(((bf16[16,256,128]{2,1,0:T(8,128)(2,1)}), bf16[16,256,128]{2,1,0:T(8,128)(2,1)S(1)}, u32[]{:S(2)}, u32[]{:S(2)}) %all-to-all-start.2) | async-done | bytes 1048608 | tf_op jit(solution)/shard_map/all_to_all | solution.py:42
  705.4 6.5 copy.203
  717.9 13.9 %all-to-all-done = bf16[16,128,256]{2,1,0:T(8,128)(2,1)S(1)} async-done(((bf16[16,128,256]{2,1,0:T(8,128)(2,1)}), bf16[16,128,256]{2,1,0:T(8,128)(2,1)S(1)}, u32[]{:S(2)}, u32[]{:S(2)}) %all-to-all-start) | async-done | bytes 1048608 | tf_op jit(solution)/shard_map/all_to_all | solution.py:42
  731.8 5.4 all-to-all-start.1
  740.7 54.6 %reduce-scatter.17.cloned.1.call-done = bf16[2,128,768]{2,1,0:T(8,128)(2,1)} async-done(((bf16[2,2048,768]{2,1,0:T(8,128)(2,1)}), bf16[2,128,768]{2,1,0:T(8,128)(2,1)}) %reduce-scatter.17.cloned.1.call-update) | async-done | bytes 393232 | tf_op jit(solution)/shard_map/reduce_scatter | solution.py:310
  807.2 76.6 %reduce-scatter.15.cloned.1.call-done = bf16[128,2048]{1,0:T(8,128)(2,1)} async-done(((bf16[1024,2048]{1,0:T(8,128)(2,1)}), bf16[128,2048]{1,0:T(8,128)(2,1)}) %reduce-scatter.15.cloned.1.call-update) | async-done | bytes 524304 | tf_op jit(solution)/shard_map/reduce_scatter | solution.py:351
  885.4 70.9 %all-reduce.5 = f32[4352]{0:T(1024)S(1)} all-reduce(f32[4352]{0:T(1024)S(1)} %pad_maximum_fusion.4), channel_id=8, replica_groups=mesh['dp'=16,'tensor'=8] {'dp','tensor'}, use_global_device_ids=true, to_apply=%region_31.32.clone | all-reduce | flops 4352 | bytes 34816
  957.0 14.6 %reduce-scatter.11.cloned.1.call-done = bf16[128,2048]{1,0:T(8,128)(2,1)} async-done(((bf16[1024,2048]{1,0:T(8,128)(2,1)}), bf16[128,2048]{1,0:T(8,128)(2,1)}) %reduce-scatter.11.cloned.1.call-update) | async-done | bytes 524304 | tf_op jit(solution)/shard_map/reduce_scatter | solution.py:295
  (302 shorter events, 143.5 us)
Async XLA Ops:
  7.2 91.0 %all-gather.8.cloned.1.call-start = ((), (), s32[]{:S(2)}) async-start(), calls=%async_computation.10 | async-start | bytes 13369344 | tf_op jit(solution)/shard_map/all_gather | solution.py:24
  13.7 157.9 %all-gather.6.cloned.1.call-start = ((), (), s32[]{:S(2)}) async-start(), calls=%async_computation.9 | async-start | bytes 4718592 | tf_op jit(solution)/shard_map/all_gather | solution.py:259
  84.7 211.8 %reduce-scatter.9.cloned.1.call-start = ((), (), s32[]{:S(2)}) async-start(), calls=%async_computation.11 | async-start | bytes 4718592 | tf_op jit(solution)/shard_map/reduce_scatter | solution.py:281
  94.7 85.1 %copy-start.42 = (f32[128]{0:T(128)}, f32[128]{0:T(128)S(1)}, u32[]{:S(2)}) copy-start(f32[128]{0:T(128)S(1)} %get-tuple-element.434) | copy-start | bytes 1540
  94.7 99.5 %copy-start.44 = (f32[128]{0:T(128)}, f32[128]{0:T(128)S(1)}, u32[]{:S(2)}) copy-start(f32[128]{0:T(128)S(1)} %get-tuple-element.435) | copy-start | bytes 1540
  214.4 156.8 %all-gather.10.cloned.1.call-start = ((), (), s32[]{:S(2)}) async-start(), calls=%async_computation.12 | async-start | bytes 4718592 | tf_op jit(solution)/shard_map/all_gather | solution.py:290
  297.8 253.5 %copy-start.46 = (f32[128]{0:T(128)}, f32[128]{0:T(128)S(1)}, u32[]{:S(2)}) copy-start(f32[128]{0:T(128)S(1)} %fusion.125) | copy-start | bytes 1540
  299.9 143.0 %all-gather.12.cloned.1.call-start = ((), (), s32[]{:S(2)}) async-start(), calls=%async_computation.14 | async-start | bytes 4718592 | tf_op jit(solution)/shard_map/all_gather | solution.py:300
  300.5 248.8 %reduce-scatter.13.cloned.1.call-start = ((), (), s32[]{:S(2)}) async-start(), calls=%async_computation.15 | async-start | bytes 4718592 | tf_op jit(solution)/shard_map/reduce_scatter | solution.py:317
  467.1 82.1 %copy-start.6 = (bf16[128,2048]{1,0:T(8,128)(2,1)S(1)}, bf16[128,2048]{1,0:T(8,128)(2,1)}, u32[]{:S(2)}) copy-start(bf16[128,2048]{1,0:T(8,128)(2,1)} %reduce-scatter.9.cloned.1.call-done) | copy-start | bytes 1572868
  467.1 84.3 %copy-start.12 = (bf16[128,2048]{1,0:T(8,128)(2,1)S(1)}, bf16[128,2048]{1,0:T(8,128)(2,1)}, u32[]{:S(2)}) copy-start(bf16[128,2048]{1,0:T(8,128)(2,1)} %param.26) | copy-start | bytes 1572868
  467.1 157.8 %all-gather.14.cloned.1.call-start = ((), (), s32[]{:S(2)}) async-start(), calls=%async_computation.16 | async-start | bytes 4718592 | tf_op jit(solution)/shard_map/all_gather | solution.py:328
  553.7 183.5 %reduce-scatter.19.cloned.1.call-start = ((), (), s32[]{:S(2)}) async-start(), calls=%async_computation.19 | async-start | bytes 3342336
  566.3 229.0 %reduce-scatter.17.cloned.1.call-start = ((), (), s32[]{:S(2)}) async-start(), calls=%async_computation.18 | async-start | bytes 6684672 | tf_op jit(solution)/shard_map/reduce_scatter | solution.py:310
  580.1 303.6 %reduce-scatter.15.cloned.1.call-start = ((), (), s32[]{:S(2)}) async-start(), calls=%async_computation.17 | async-start | bytes 4718592 | tf_op jit(solution)/shard_map/reduce_scatter | solution.py:351
  664.0 307.6 %reduce-scatter.11.cloned.1.call-start = ((), (), s32[]{:S(2)}) async-start(), calls=%async_computation.13 | async-start | bytes 4718592 | tf_op jit(solution)/shard_map/reduce_scatter | solution.py:295
  677.7 23.3 %all-to-all-start.2 = ((bf16[16,256,128]{2,1,0:T(8,128)(2,1)}), bf16[16,256,128]{2,1,0:T(8,128)(2,1)S(1)}, u32[]{:S(2)}, u32[]{:S(2)}) async-start(bf16[16,256,128]{2,1,0:T(8,128)(2,1)} %bitcast.295), calls=%async_computation.6 | async-start | bytes 2097152 | tf_op jit(solution)/shard_map/all_to_all | solution.py:42
  701.0 30.8 %all-to-all-start = ((bf16[16,128,256]{2,1,0:T(8,128)(2,1)}), bf16[16,128,256]{2,1,0:T(8,128)(2,1)S(1)}, u32[]{:S(2)}, u32[]{:S(2)}) async-start(bf16[16,128,256]{2,1,0:T(8,128)(2,1)} %bitcast.385), calls=%async_computation.4 | async-start | bytes 2097152 | tf_op jit(solution)/shard_map/all_to_all | solution.py:42
  731.8 68.6 %all-to-all-start.1 = ((bf16[16,2,128,128]{3,2,1,0:T(8,128)(2,1)}), bf16[16,2,128,128]{3,2,1,0:T(8,128)(2,1)}, u32[]{:S(2)}, u32[]{:S(2)}) async-start(bf16[16,2,128,128]{3,2,1,0:T(8,128)(2,1)} %copy.192), calls=%async_computation.5 | async-start | bytes 2097152 | tf_op jit(solution)/shard_map/all_to_all | solution.py:42
  798.6 85.2 %copy-start.34 = (f32[2048]{0:T(1024)S(1)}, f32[2048]{0:T(1024)}, u32[]{:S(2)}) copy-start(f32[2048]{0:T(1024)} %copy-done.33) | copy-start | bytes 24580
  798.6 173.0 %copy-start.13 = (bf16[128,2048]{1,0:T(8,128)(2,1)S(1)}, bf16[128,2048]{1,0:T(8,128)(2,1)}, u32[]{:S(2)}) copy-start(bf16[128,2048]{1,0:T(8,128)(2,1)} %param.26) | copy-start | bytes 1572868
  798.6 173.0 %copy-start.14 = (bf16[128,2048]{1,0:T(8,128)(2,1)S(1)}, bf16[128,2048]{1,0:T(8,128)(2,1)}, u32[]{:S(2)}) copy-start(bf16[128,2048]{1,0:T(8,128)(2,1)} %reduce-scatter.13.cloned.1.call-done) | copy-start | bytes 1572868
  798.8 85.0 %copy-start.49 = (f32[128]{0:T(128)S(1)}, f32[128]{0:T(128)}, u32[]{:S(2)}) copy-start(f32[128]{0:T(128)} %copy-done.48) | copy-start | bytes 1540
  798.8 86.6 %copy-start.39 = (f32[2048]{0:T(1024)S(1)}, f32[2048]{0:T(1024)}, u32[]{:S(2)}) copy-start(f32[2048]{0:T(1024)} %get-tuple-element.334) | copy-start | bytes 24580
  798.8 86.6 %copy-start.50 = (f32[128]{0:T(128)S(1)}, f32[128]{0:T(128)}, u32[]{:S(2)}) copy-start(f32[128]{0:T(128)} %get-tuple-element.340) | copy-start | bytes 1540
  798.8 86.6 %copy-start.51 = (f32[128]{0:T(128)S(1)}, f32[128]{0:T(128)}, u32[]{:S(2)}) copy-start(f32[128]{0:T(128)} %get-tuple-element.338) | copy-start | bytes 1540
  798.8 157.6 %copy-start.55 = (f32[128]{0:T(128)S(1)}, f32[128]{0:T(128)}, u32[]{:S(2)}) copy-start(f32[128]{0:T(128)} %copy-done.54) | copy-start | bytes 1540
  798.8 157.6 %copy-start.58 = (f32[34]{0:T(128)S(1)}, f32[34]{0:T(128)}, u32[]{:S(2)}) copy-start(f32[34]{0:T(128)} %param.33) | copy-start | bytes 412
  798.8 157.6 %copy-start.59 = (f32[34]{0:T(128)S(1)}, f32[34]{0:T(128)}, u32[]{:S(2)}) copy-start(f32[34]{0:T(128)} %param.45) | copy-start | bytes 412
  798.8 157.6 %copy-start.60 = (f32[34]{0:T(128)S(1)}, f32[34]{0:T(128)}, u32[]{:S(2)}) copy-start(f32[34]{0:T(128)} %param.39) | copy-start | bytes 412
  798.8 172.8 %copy-start.47 = (f32[128]{0:T(128)S(1)}, f32[128]{0:T(128)}, u32[]{:S(2)}) copy-start(f32[128]{0:T(128)} %copy-done.46) | copy-start | bytes 1540
  798.9 172.8 %copy-start.53 = (f32[128]{0:T(128)S(1)}, f32[128]{0:T(128)}, u32[]{:S(2)}) copy-start(f32[128]{0:T(128)} %copy-done.52) | copy-start | bytes 1540
  (55 other events, 532.9 us)
Sparse Core Ops, SparseCore 0:
  13.8 84.4 all-gather.7
  101.2 70.3 all-gather.5
  214.5 81.9 reduce-scatter.8
  300.0 71.1 all-gather.9
  373.4 69.4 all-gather.11
  467.2 81.9 reduce-scatter.12
  553.8 71.1 all-gather.13
  627.4 62.5 reduce-scatter.18
  692.4 102.8 reduce-scatter.16
  799.0 84.7 reduce-scatter.14
  887.7 83.9 reduce-scatter.10
where the time goes:
time: 986 us; the launch traced here: 981 us
  waiting for transfers between devices  570 us (58%)
  blocking collectives  140 us (14%)
  matrix products  120 us (12%)
  other arithmetic  66.3 us (7%)
  local copies, waits for them, and re-layouts  53.4 us (5%)
  starting transfers between devices  16.1 us (2%)
  between operations  15.1 us (2%)
    unnamed x2, blocking collectives  140 us
    reduce_scatter x1, waiting for transfers between devices, body(): lax.psum_scatter((contract_last(gate_low, gateup_back[0]) + contract_last...  82.1 us
    reduce_scatter x1, waiting for transfers between devices, body(): lax.psum_scatter(product(attended_low, output_full).astype(jnp.bfloat16),...  82 us
    reduce_scatter x1, waiting for transfers between devices, body(): lax.psum_scatter((contract_last(query_low, query_back) + contract_last(ke...  76.6 us
    all_gather x1, waiting for transfers between devices, body(): portion = lax.all_gather(first_low, 'tensor', axis=0, tiled=True)  71.3 us
    all_gather x1, waiting for transfers between devices, body(): upstream_all = lax.all_gather(cotangent, 'tensor', axis=0, tiled=True)  58.1 us
    all_gather x1, waiting for transfers between devices, body(): portion = lax.all_gather(second_low, 'tensor', axis=0, tiled=True)  55.2 us
    reduce_scatter x1, waiting for transfers between devices, body(): lax.psum_scatter(gateup_grad.astype(jnp.bfloat16), 'dp', scatter_dimensio...  54.6 us
  transfers between devices with their start and end apart: 14, of which 12 were waited for; matrix products, arithmetic and copies ran while one was open for 16% of the time, Pallas kernels for 0%

commit v1 on v0

v1 whole, which is shorter than its diff:
```python
import math

import jax
import jax.numpy as jnp
from jax import lax
from jax.experimental import pallas as pl
from jax.experimental.pallas import tpu as pltpu
from jax.sharding import Mesh
from jax.sharding import PartitionSpec as P

MODEL_WIDTH = 2048
QUERY_HEADS = 16
HEAD_SIZE = 128
FF = 6144
EPSILON = 1e-06
MOMENTUM = 0.9
AVERAGING = 0.5
ROPE_BASE = 1000000.0

AXES = ("z", "ylo", "core", "yhi", "x")
GRID = (4, 2, 2, 2, 4)
RING = 4
BF16 = jnp.bfloat16
F32 = jnp.float32


class Place:
    def __init__(self):
        self.x = lax.axis_index("x")
        self.z = lax.axis_index("z")
        self.core = lax.axis_index("core")
        self.yhi = lax.axis_index("yhi")
        self.ylo = lax.axis_index("ylo")
        self.y = self.yhi * 2 + self.ylo

    def at(self, axis):
        return self.x if axis == "x" else self.y if axis == "y" else self.z

    def step(self, axis, by):
        return lax.rem(self.at(axis) + (by + RING), RING)

    def device(self, axis, by=1):
        if axis == "core":
            return {"core": 1 - self.core}
        if axis == "turn":
            return {"core": 1 - self.core, "yhi": 1 - self.yhi}
        there = self.step(axis, by)
        if axis == "y":
            return {"yhi": lax.div(there, 2), "ylo": lax.rem(there, 2)}
        return {axis: there}

    def native(self):
        return self.core == self.yhi


class Net:
    def __init__(self, place, send_sems, recv_sems, local_sems):
        self.place = place
        self.send_sems, self.recv_sems, self.local_sems = send_sems, recv_sems, local_sems
        self.count = 0
        self.local_count = 0
        self.pending = []
        self.late = []

    def copy(self, source, target, index, axis, by=1):
        return pltpu.make_async_remote_copy(
            src_ref=source,
            dst_ref=target,
            send_sem=self.send_sems.at[index],
            recv_sem=self.recv_sems.at[index],
            device_id=self.place.device(axis, by),
            device_id_type=pl.DeviceIdType.MESH,
        )

    def number(self):
        self.count += 1
        return self.count - 1

    def send(self, source, target, axis, by=1):
        index = self.number()
        copy = self.copy(source, target, index, axis, by)
        copy.start()
        self.pending.append(copy)
        return index

    def arrive(self, index, target, axis, by=1):
        self.copy(target, target, index, axis, by).wait_recv()

    def local(self, source, target):
        copy = pltpu.make_async_copy(source, target, self.local_sems.at[self.local_count])
        self.local_count += 1
        copy.start()
        return copy

    def finish(self):
        for wait in self.late:
            wait()
        for copy in self.pending:
            copy.wait_send()


def greet(place, partners):
    barrier = pltpu.get_barrier_semaphore()
    for axis, by in partners:
        pl.semaphore_signal(
            barrier,
            inc=1,
            device_id=place.device(axis, by),
            device_id_type=pl.DeviceIdType.MESH,
        )
    pl.semaphore_wait(barrier, len(partners))


def drive(parts):
    parts = list(parts)
    while parts:
        for part in list(parts):
            try:
                next(part)
            except StopIteration:
                parts.remove(part)


def rows_gather(net, own, whole, rows):
    place = net.place
    half = rows // 2

    def block(core, x, part):
        start = pl.multiple_of((core * RING + x) * rows + part * half, half)
        return whole.at[pl.ds(start, half)]

    me, other = place.core, 1 - place.core
    right, left, far = place.step("x", 1), place.step("x", -1), place.step("x", 2)
    kept = net.local(own, whole.at[pl.ds(pl.multiple_of((me * RING + place.x) * rows, rows), rows)])
    piece = [own.at[pl.ds(part * half, half)] for part in range(2)]
    sent = {}
    for axis, by, part in (("x", 1, 0), ("x", -1, 1), ("x", 1, 1), ("x", -1, 0)):
        sent[by, part] = net.send(piece[part], block(me, place.x, part), axis, by)
    shared = []

    def share(x, part, source=None):
        there = block(me, x, part)
        shared.append((net.send(there if source is None else source, there, "core"), x, part))

    share(place.x, 0, piece[0])
    share(place.x, 1, piece[1])
    yield
    net.arrive(sent[1, 0], block(me, left, 0), "x", 1)
    passed_right = net.send(block(me, left, 0), block(me, left, 0), "x", 1)
    share(left, 0)
    net.arrive(sent[-1, 1], block(me, right, 1), "x", -1)
    passed_left = net.send(block(me, right, 1), block(me, right, 1), "x", -1)
    share(right, 1)
    yield
    net.arrive(sent[1, 1], block(me, left, 1), "x", 1)
    share(left, 1)
    net.arrive(sent[-1, 0], block(me, right, 0), "x", -1)
    share(right, 0)
    yield
    net.arrive(passed_right, block(me, far, 0), "x", 1)
    share(far, 0)
    net.arrive(passed_left, block(me, far, 1), "x", -1)
    share(far, 1)
    yield
    for index, x, part in shared:
        net.arrive(index, block(other, x, part), "core")
    kept.wait()


ROWS_GATHER_COPIES = 14


def ring_sum(net, axis, own, land, finish):
    through_left, through_right, sum_right, sum_left = land[0], land[1], land[2], land[3]
    from_left, from_right = (land[4], land[5]), (land[6], land[7])
    a = net.send(own(2, 0), through_left, axis, 1)
    b = net.send(own(2, 1), through_right, axis, -1)
    c = net.send(own(1, 1), from_left[1], axis, 1)
    d = net.send(own(-1, 0), from_right[0], axis, -1)
    yield
    net.arrive(a, through_left, axis, 1)
    sum_right[...] = through_left[...] + own(1, 0)[...]
    e = net.send(sum_right, from_left[0], axis, 1)
    net.arrive(b, through_right, axis, -1)
    sum_left[...] = through_right[...] + own(-1, 1)[...]
    f = net.send(sum_left, from_right[1], axis, -1)
    yield
    net.arrive(d, from_right[0], axis, -1)
    net.arrive(c, from_left[1], axis, 1)
    net.arrive(e, from_left[0], axis, 1)
    net.arrive(f, from_right[1], axis, -1)
    for part in range(2):
        total = own(0, part)[...].astype(F32) + from_left[part][...].astype(F32)
        finish(part, total + from_right[part][...].astype(F32))
    yield


RING_SUM_COPIES = 6


def rows_sum(net, whole, total, rows, landed, summed, land):
    place = net.place
    half = rows // 2

    def block(core, x, part):
        start = pl.multiple_of((core * RING + x) * rows + part * half, half)
        return whole.at[pl.ds(start, half)]

    me, other = place.core, 1 - place.core
    order = [(2, 0), (2, 1), (1, 1), (-1, 0), (1, 0), (-1, 1), (0, 0), (0, 1)]
    sent = [
        net.send(block(other, place.step("x", k), part), landed.at[k % RING, part], "core")
        for k, part in order
    ]
    yield
    def combine(at):
        k, part = order[at]
        net.arrive(sent[at], landed.at[k % RING, part], "core")
        summed[k % RING, part] = block(me, place.step("x", k), part)[...] + landed[k % RING, part]

    for at in range(4):
        combine(at)

    def own(k, part):
        return summed.at[k % RING, part]

    def finish(part, value):
        total[pl.ds(part * half, half)] = value

    ring = ring_sum(net, "x", own, [land.at[n] for n in range(8)], finish)
    next(ring)
    for at in range(4, 8):
        combine(at)
    yield
    yield from ring


ROWS_SUM_COPIES = 8 + RING_SUM_COPIES


def plane_gather(net, own, whole, rows, spot):
    place = net.place
    quarter = rows // 4

    def view(z, y, color, part):
        row, columns = spot(z, y)
        start = pl.multiple_of(row + (color * 2 + part) * quarter, quarter)
        return whole.at[pl.ds(start, quarter), columns]

    def one(color):
        first, second = ("z", "y") if color == 0 else ("y", "z")

        def at(i, j, part):
            z, y = (i, j) if color == 0 else (j, i)
            return view(z, y, color, part)

        def ring(axis, here, sources):
            sent = {}
            for by, part in ((1, 0), (-1, 1), (1, 1), (-1, 0)):
                source = sources[part] if sources is not None else here(place.at(axis), part)
                sent[by, part] = net.send(source, here(place.at(axis), part), axis, by)
            yield
            left, right, far = place.step(axis, -1), place.step(axis, 1), place.step(axis, 2)
            net.arrive(sent[1, 0], here(left, 0), axis, 1)
            go = net.send(here(left, 0), here(left, 0), axis, 1)
            net.arrive(sent[-1, 1], here(right, 1), axis, -1)
            back = net.send(here(right, 1), here(right, 1), axis, -1)
            net.arrive(sent[1, 1], here(left, 1), axis, 1)
            net.arrive(sent[-1, 0], here(right, 0), axis, -1)
            yield
            net.arrive(go, here(far, 0), axis, 1)
            net.arrive(back, here(far, 1), axis, -1)
            yield

        mine = [own.at[pl.ds((color * 2 + part) * quarter, quarter)] for part in range(2)]
        one_ring = ring(first, lambda i, part: at(i, place.at(second), part), mine)

        def second_ring(k):
            i = place.step(first, k)
            return ring(
                second, lambda j, part: at(i, j, part), mine if k == 0 else None
            )

        rings = [second_ring(0)]
        next(one_ring)
        next(rings[0])
        yield
        next(one_ring)
        for k in (1, -1):
            rings.append(second_ring(k))
            next(rings[-1])
        yield
        next(rings[0])
        next(one_ring)
        rings.append(second_ring(2))
        next(rings[-1])
        yield
        next(rings[1])
        next(rings[2])
        yield
        next(rings[3])
        yield
        for ring_ in rings:
            next(ring_)
        yield

    row, columns = spot(place.z, place.y)
    kept = net.local(own, whole.at[pl.ds(pl.multiple_of(row, rows), rows), columns])
    parts = [one(0), one(1)]
    for _ in range(6):
        for part in parts:
            next(part)
        yield
    kept.wait()


PLANE_GATHER_COPIES = 60


def plane_sum(net, whole, total, rows, spot, land, between):
    place = net.place
    quarter = rows // 4

    def view(z, y, color, part):
        row, columns = spot(z, y)
        start = pl.multiple_of(row + (color * 2 + part) * quarter, quarter)
        return whole.at[pl.ds(start, quarter), columns]

    def one(color):
        first, second = ("y", "z") if color == 0 else ("z", "y")

        def first_ring(k):
            def own(n, part):
                far, near = place.step(second, k), place.step(first, n)
                z, y = (far, near) if color == 0 else (near, far)
                return view(z, y, color, part)

            def keep(part, value):
                between[color, k % RING, part] = value.astype(BF16)

            slots = [land.at[color, k % RING, n] for n in range(8)]
            return ring_sum(net, first, own, slots, keep)

        rings = [first_ring(k) for k in (2, 1, -1, 0)]
        for ring in rings:
            next(ring)
        yield
        for ring in rings:
            next(ring)
        yield
        for ring in rings[:3]:
            next(ring)

        def done(part, value):
            start = (color * 2 + part) * quarter
            total[pl.ds(start, quarter)] = value.astype(total.dtype)

        last = ring_sum(
            net,
            second,
            lambda k, part: between.at[color, k % RING, part],
            [land.at[color, 4, n] for n in range(8)],
            done,
        )
        next(last)
        next(rings[3])
        yield
        next(last)
        yield
        next(last)
        yield

    parts = [one(0), one(1)]
    for _ in range(5):
        for part in parts:
            next(part)
        yield


PLANE_SUM_COPIES = 2 * 5 * RING_SUM_COPIES


def turned(net, pairs):
    place = net.place
    native = place.native()
    firsts = [(net.number(), net.number()) for _ in pairs]
    base = net.local_count
    net.local_count += len(pairs)

    def halves(ref):
        rows = ref.shape[0] // 2
        return [ref.at[pl.ds(part * rows, rows)] for part in range(2)]

    def copies():
        return [
            net.copy(source, target, index, "turn")
            for (whole_source, whole_target), indices in zip(pairs, firsts)
            for source, target, index in zip(halves(whole_source), halves(whole_target), indices)
        ]

    def kept():
        return [
            pltpu.make_async_copy(source, target, net.local_sems.at[base + k])
            for k, (source, target) in enumerate(pairs)
        ]

    @pl.when(jnp.logical_not(native))
    def _():
        for copy in copies():
            copy.start()

    @pl.when(native)
    def _():
        for copy in kept():
            copy.start()

    yield

    def wait_all():
        @pl.when(jnp.logical_not(native))
        def _():
            for copy in copies():
                copy.wait()

        @pl.when(native)
        def _():
            for copy in kept():
                copy.wait()

    net.late.append(wait_all)


def gains_gather(net, own, whole):
    place = net.place

    def rows(z, y, x, core, count):
        start = ((z * RING + y) * RING + x) * 2 + core
        return whole.at[pl.ds(start if count == 1 else pl.multiple_of(start, count), count)]

    kept = net.local(own, rows(place.z, place.y, place.x, place.core, 1))
    kept.wait()
    spots = {
        "core": lambda by: rows(place.z, place.y, place.x, (place.core + by) % 2, 1),
        "x": lambda by: rows(place.z, place.y, place.step("x", by), 0, 2),
        "y": lambda by: rows(place.z, place.step("y", by), 0, 0, 8),
        "z": lambda by: rows(place.step("z", by), 0, 0, 0, 32),
    }
    for axis in ("core", "x", "y", "z"):
        spot = spots[axis]
        steps = (1,) if axis == "core" else (1, -1, 2)
        sent = [net.send(spot(0), spot(0), axis, by) for by in steps]
        yield
        for index, by in zip(sent, steps):
            net.arrive(index, spot(-by), axis, by)
    yield


GAINS_COPIES = 10


def gains_sum(net, whole, total, land):
    place = net.place

    def rows(z, y, x, core, count):
        start = ((z * RING + y) * RING + x) * 2 + core
        return whole.at[pl.ds(start if count == 1 else pl.multiple_of(start, count), count)]

    spots = {
        "z": lambda by: rows(place.step("z", by), 0, 0, 0, 32),
        "y": lambda by: rows(place.z, place.step("y", by), 0, 0, 8),
        "x": lambda by: rows(place.z, place.y, place.step("x", by), 0, 2),
        "core": lambda by: rows(place.z, place.y, place.x, (place.core + by) % 2, 1),
    }
    first = 0
    for axis, count in (("z", 32), ("y", 8), ("x", 2), ("core", 1)):
        spot = spots[axis]
        steps = (1,) if axis == "core" else (1, -1, 2)
        sent = [
            net.send(spot(by), land.at[n, pl.ds(first, count)], axis, by)
            for n, by in enumerate(steps)
        ]
        yield
        value = spot(0)[...]
        for n, (index, by) in enumerate(zip(sent, steps)):
            net.arrive(index, land.at[n, pl.ds(first, count)], axis, by)
            value = value + land[n, pl.ds(first, count)]
        if axis == "core":
            total[...] = value
        else:
            spot(0)[...] = value
        first += count
    yield


class Kernel:
    def __init__(self, number, copies, locals_, partners):
        self.number, self.copies, self.locals_, self.partners = number, copies, locals_, partners

    def __call__(self, plan, arrays, outs, scratch=()):
        spaces = [pl.BlockSpec(memory_space=space) for _, space in arrays]
        n_in, n_out, n_scratch = len(arrays), len(outs), len(scratch)

        def kernel(*refs):
            ins, results = refs[:n_in], refs[n_in : n_in + n_out]
            work = refs[n_in + n_out : n_in + n_out + n_scratch]
            place = Place()
            net = Net(place, *refs[n_in + n_out + n_scratch :])
            greet(place, self.partners)
            drive(plan(net, ins, results, work))
            net.finish()

        return pl.pallas_call(
            kernel,
            out_shape=[shape for shape, _ in outs],
            in_specs=spaces,
            out_specs=[pl.BlockSpec(memory_space=space) for _, space in outs],
            scratch_shapes=[
                *scratch,
                pltpu.SemaphoreType.DMA((self.copies,)),
                pltpu.SemaphoreType.DMA((self.copies,)),
                pltpu.SemaphoreType.DMA((self.locals_,)),
            ],
            compiler_params=pltpu.CompilerParams(
                collective_id=self.number, has_side_effects=True, vmem_limit_bytes=48 * 2**20
            ),
            name="links_%d" % self.number,
        )(*[array for array, _ in arrays])


HBM = pl.ANY
VMEM = pltpu.VMEM
X_PARTNERS = (("x", 1), ("x", -1), ("core", 1))
PLANE_PARTNERS = (("y", 1), ("y", -1), ("z", 1), ("z", -1))
TURN_PARTNERS = (("turn", 1),)


def shape(dims, dtype=BF16):
    return jax.ShapeDtypeStruct(dims, dtype)


def attention_spot(z, y):
    piece = z * 4 + lax.rem(y, 2) * 2 + lax.div(y, 2)
    return piece * 128


def rows_spot(z, y):
    return attention_spot(z, y), pl.ds(0, 512)


def output_spot(z, y):
    return 0, pl.ds(pl.multiple_of(attention_spot(z, y), 128), 128)


def gateup_spot(z, y):
    columns = pl.ds(pl.multiple_of(lax.div(y, 2) * 384, 128), 384)
    return (z * 2 + lax.rem(y, 2)) * 256, columns


def down_spot(z, y):
    columns = pl.ds(pl.multiple_of((z * 2 + lax.rem(y, 2)) * 256, 128), 256)
    return lax.div(y, 2) * 384, columns


def enter(tokens, qkv, output, gains, lengths):
    def plan(net, ins, outs, work):
        tokens_, qkv_, output_, gains_, lengths_ = ins

        def swap_lengths():
            index = net.send(lengths_, outs[4], "core")
            yield
            net.arrive(index, outs[4], "core")

        return [
            gains_gather(net, gains_, outs[3]),
            turned(net, [(tokens_, outs[0]), (qkv_, outs[1]), (output_, outs[2])]),
            swap_lengths(),
        ]

    partners = X_PARTNERS + (("x", 2),) + PLANE_PARTNERS + (("y", 2), ("z", 2)) + TURN_PARTNERS
    return Kernel(0, GAINS_COPIES + 6 + 1, 4, partners)(
        plan,
        [(tokens, HBM), (qkv, HBM), (output, HBM), (gains, VMEM), (lengths, VMEM)],
        [
            (shape(tokens.shape), HBM),
            (shape(qkv.shape), HBM),
            (shape(output.shape), HBM),
            (shape((128, 1, 128), F32), VMEM),
            (shape((8, 128), jnp.int32), VMEM),
        ],
    )


def first_gather(first_low, qkv, output, cotangent, gate, up, down):
    def plan(net, ins, outs, work):
        first_, qkv_, output_, cotangent_, gate_, up_, down_ = ins
        place = net.place
        mine, theirs = place.core, 1 - place.core

        def halves():
            kept, sent = [], []
            for source, target in ((gate_, outs[4]), (up_, outs[5])):
                spot = target.at[pl.ds(pl.multiple_of(mine * 128, 128), 128)]
                there = target.at[pl.ds(pl.multiple_of(theirs * 128, 128), 128)]
                cut = lambda core: source.at[:, pl.ds(pl.multiple_of(core * 384, 128), 384)]
                kept.append(net.local(cut(mine), spot))
                sent.append((net.send(cut(theirs), spot, "core"), there))
            spot = outs[6].at[:, pl.ds(pl.multiple_of(mine * 128, 128), 128)]
            there = outs[6].at[:, pl.ds(pl.multiple_of(theirs * 128, 128), 128)]
            cut = lambda core: down_.at[pl.ds(pl.multiple_of(core * 384, 128), 384)]
            kept.append(net.local(cut(mine), spot))
            sent.append((net.send(cut(theirs), spot, "core"), there))
            yield
            for copy in kept:
                copy.wait()
            for index, there in sent:
                net.arrive(index, there, "core")

        return [
            rows_gather(net, first_, outs[0], 128),
            plane_gather(net, qkv_, outs[1], 128, rows_spot),
            plane_gather(net, output_, outs[2], 256, output_spot),
            turned(net, [(cotangent_, outs[3])]),
            halves(),
        ]

    return Kernel(
        1, ROWS_GATHER_COPIES + 2 * PLANE_GATHER_COPIES + 2 + 3, 1 + 2 + 1 + 3,
        X_PARTNERS + PLANE_PARTNERS + TURN_PARTNERS,
    )(
        plan,
        [(a, HBM) for a in (first_low, qkv, output, cotangent, gate, up, down)],
        [
            (shape((1024, 2048)), HBM),
            (shape((2048, 512)), HBM),
            (shape((256, 2048)), HBM),
            (shape((128, 2048)), HBM),
            (shape((256, 384)), HBM),
            (shape((256, 384)), HBM),
            (shape((384, 256)), HBM),
        ],
    )


def gather_and_weight(number, rows, piece, whole, spot):
    def plan(net, ins, outs, work):
        return [
            rows_gather(net, ins[0], outs[0], 128),
            plane_gather(net, ins[1], outs[1], piece.shape[0], spot),
        ]

    return Kernel(
        number, ROWS_GATHER_COPIES + PLANE_GATHER_COPIES, 2, X_PARTNERS + PLANE_PARTNERS
    )(
        plan,
        [(rows, HBM), (piece, HBM)],
        [(shape((1024, 2048)), HBM), (shape(whole), HBM)],
    )


SUM_SCRATCH = (
    pltpu.VMEM((4, 2, 64, 2048), BF16),
    pltpu.VMEM((4, 2, 64, 2048), BF16),
    pltpu.VMEM((8, 64, 2048), BF16),
)


def plane_scratch(rows, columns):
    return (
        pltpu.VMEM((2, 5, 8, rows // 4, columns), BF16),
        pltpu.VMEM((2, 4, 2, rows // 4, columns), BF16),
    )


def sum_and_weight(number, terms, piece, whole, spot):
    def plan(net, ins, outs, work):
        return [
            rows_sum(net, ins[0], outs[0], 128, *work),
            plane_gather(net, ins[1], outs[1], piece.shape[0], spot),
        ]

    return Kernel(
        number, ROWS_SUM_COPIES + PLANE_GATHER_COPIES, 1, X_PARTNERS + PLANE_PARTNERS
    )(
        plan,
        [(terms, VMEM), (piece, HBM)],
        [(shape((128, 2048), F32), VMEM), (shape(whole), HBM)],
        SUM_SCRATCH,
    )


def sum_and_gradient(number, terms, gradient, piece, spot):
    def plan(net, ins, outs, work):
        return [
            rows_sum(net, ins[0], outs[0], 128, *work[:3]),
            plane_sum(net, ins[1], outs[1], piece[0], spot, *work[3:]),
        ]

    return Kernel(
        number, ROWS_SUM_COPIES + PLANE_SUM_COPIES, 1, X_PARTNERS + PLANE_PARTNERS
    )(
        plan,
        [(terms, VMEM), (gradient, VMEM)],
        [(shape((128, 2048), F32), VMEM), (shape(piece), VMEM)],
        SUM_SCRATCH + plane_scratch(*piece),
    )


def gather_and_gradient(number, rows, gradient, piece, spot):
    def plan(net, ins, outs, work):
        return [
            rows_gather(net, ins[0], outs[0], 128),
            plane_sum(net, ins[1], outs[1], piece[0], spot, *work),
        ]

    return Kernel(
        number, ROWS_GATHER_COPIES + PLANE_SUM_COPIES, 1, X_PARTNERS + PLANE_PARTNERS
    )(
        plan,
        [(rows, HBM), (gradient, VMEM)],
        [(shape((1024, 2048)), HBM), (shape(piece), VMEM)],
        plane_scratch(*piece),
    )


def last_sums(terms, qkv_grad, output_grad, gains):
    def plan(net, ins, outs, work):
        return [
            rows_sum(net, ins[0], outs[0], 128, *work[:3]),
            plane_sum(net, ins[1], outs[1], 128, rows_spot, *work[3:5]),
            plane_sum(net, ins[2], outs[2], 256, output_spot, *work[5:7]),
            gains_sum(net, work[8], outs[3], work[7]),
        ]

    def with_gains(net, ins, outs, work):
        net.local(ins[3], work[8]).wait()
        return plan(net, ins, outs, work)

    return Kernel(
        8, ROWS_SUM_COPIES + 2 * PLANE_SUM_COPIES + GAINS_COPIES, 1,
        X_PARTNERS + (("x", 2),) + PLANE_PARTNERS + (("y", 2), ("z", 2)),
    )(
        with_gains,
        [(terms, VMEM), (qkv_grad, VMEM), (output_grad, VMEM), (gains, HBM)],
        [
            (shape((128, 2048), F32), VMEM),
            (shape((128, 512)), VMEM),
            (shape((256, 128)), VMEM),
            (shape((1, 1, 128), F32), VMEM),
        ],
        SUM_SCRATCH
        + plane_scratch(128, 512)
        + plane_scratch(256, 128)
        + (pltpu.VMEM((3, 64, 1, 128), F32), pltpu.VMEM((128, 1, 128), F32)),
    )


def leave(block_out, input_grad, qkv, output, gate, up, down):
    def plan(net, ins, outs, work):
        place = net.place
        mine, theirs = place.core, 1 - place.core

        def halves():
            kept, sent = [], []
            for source, target in ((ins[4], outs[4]), (ins[5], outs[5])):
                cut = lambda core: source.at[pl.ds(pl.multiple_of(core * 128, 128), 128)]
                spot = target.at[:, pl.ds(pl.multiple_of(mine * 384, 128), 384)]
                there = target.at[:, pl.ds(pl.multiple_of(theirs * 384, 128), 384)]
                kept.append(net.local(cut(mine), spot))
                sent.append((net.send(cut(theirs), spot, "core"), there))
            cut = lambda core: ins[6].at[:, pl.ds(pl.multiple_of(core * 128, 128), 128)]
            spot = outs[6].at[pl.ds(pl.multiple_of(mine * 384, 128), 384)]
            there = outs[6].at[pl.ds(pl.multiple_of(theirs * 384, 128), 384)]
            kept.append(net.local(cut(mine), spot))
            sent.append((net.send(cut(theirs), spot, "core"), there))
            yield
            for copy in kept:
                copy.wait()
            for index, there in sent:
                net.arrive(index, there, "core")

        return [turned(net, list(zip(ins[:4], outs[:4]))), halves()]

    return Kernel(9, 8 + 3, 4 + 3, (("core", 1),) + TURN_PARTNERS)(
        plan,
        [(a, HBM) for a in (block_out, input_grad, qkv, output, gate, up, down)],
        [
            (shape((128, 2048)), HBM),
            (shape((128, 2048)), HBM),
            (shape((128, 512)), HBM),
            (shape((256, 128)), HBM),
            (shape((128, 768)), HBM),
            (shape((128, 768)), HBM),
            (shape((768, 128)), HBM),
        ],
    )


def root_mean_norm(value_vectors, scaling):
    return (
        value_vectors
        * lax.rsqrt(jnp.mean(value_vectors * value_vectors, axis=-1, keepdims=True) + EPSILON)
        * scaling
    )


def rotary_embed(value_vectors, cosine_table, sine_table):
    middle = value_vectors.shape[-1] // 2
    turned = jnp.concatenate([-value_vectors[..., middle:], value_vectors[..., :middle]], axis=-1)
    return value_vectors * cosine_table + turned * sine_table


def doc_layout(length_row, row_total_count):
    doc_ends = jnp.cumsum(length_row)
    places = jnp.arange(row_total_count, dtype=jnp.int32)
    passed = places[:, None] >= doc_ends[None, :]
    segment = jnp.sum(passed.astype(jnp.int32), axis=1)
    starts = jnp.sum(jnp.where(passed, length_row[None, :], 0), axis=1)
    position = places - starts
    halves = jnp.arange(HEAD_SIZE // 2, dtype=jnp.float32)
    inverse = ROPE_BASE ** (-2.0 * halves / HEAD_SIZE)
    angles = position.astype(jnp.float32)[:, None] * inverse[None, :]
    angles = jnp.concatenate([angles, angles], axis=-1)
    return (segment, places, jnp.cos(angles), jnp.sin(angles))


def step_rates(total_tokens):
    root_tokens = math.sqrt(total_tokens)
    narrow = MODEL_WIDTH ** (-0.5)
    return (
        narrow / (2.0 * root_tokens),
        narrow / (2.0 * root_tokens),
        (QUERY_HEADS * HEAD_SIZE // 128) ** (-0.5) / (0.24 * root_tokens),
        narrow / (0.7 * root_tokens),
        FF ** (-0.5) / (1.2 * root_tokens),
        0.025 / root_tokens,
    )


def swiglu(gate_value, upward):
    return jax.nn.silu(gate_value) * upward


def head_turn(projected, scaling, cosine_table, sine_table):
    heads = projected.reshape(projected.shape[0], -1, HEAD_SIZE)
    return rotary_embed(
        root_mean_norm(heads, scaling), cosine_table[:, None, :], sine_table[:, None, :]
    )


def product(left, right):
    return jnp.dot(left, right, preferred_element_type=jnp.float32)


def contract_last(left, right):
    return lax.dot_general(
        left, right, (((1,), (1,)), ((), ())), preferred_element_type=jnp.float32
    )


def contract_first(left, right):
    return lax.dot_general(
        left, right, (((0,), (0,)), ((), ())), preferred_element_type=jnp.float32
    )


def scores_for(query_tile_block, key_vectors):
    return jnp.einsum(
        "qkgd,skd->kgqs", query_tile_block, key_vectors, preferred_element_type=jnp.float32
    ) * HEAD_SIZE ** (-0.5)


def mask_for(segment_block, place_block, segment, places):
    return (segment_block[:, None] == segment[None, :]) & (places[None, :] <= place_block[:, None])


def attend_forward(queries, key_vectors, value_vectors, segment, places, block_row_span):
    row_total_count = queries.shape[0]
    key_heads = key_vectors.shape[1]
    sharing = queries.shape[1] // key_heads
    blocks = row_total_count // block_row_span
    grouped_heads = queries.reshape(blocks, block_row_span, key_heads, sharing, HEAD_SIZE)

    def one_block(element):
        query_tile_block, segment_block, place_block = element
        allowed = mask_for(segment_block, place_block, segment, places)
        scores = jnp.where(allowed, scores_for(query_tile_block, key_vectors), -1e30)
        highest = jnp.max(scores, axis=-1, keepdims=True)
        weights = jnp.exp(scores - highest)
        summed = jnp.sum(weights, axis=-1, keepdims=True)
        probability = (weights / summed).astype(jnp.bfloat16)
        blended = jnp.einsum(
            "kgqs,skd->qkgd", probability, value_vectors, preferred_element_type=jnp.float32
        )
        return (blended.reshape(block_row_span, -1), highest + jnp.log(summed))

    return lax.map(
        one_block,
        (
            grouped_heads,
            segment.reshape(blocks, block_row_span),
            places.reshape(blocks, block_row_span),
        ),
    )


def attend_backward(
    queries, key_vectors, value_vectors, out_grad, log_totals, segment, places, block_row_span
):
    row_total_count = queries.shape[0]
    key_heads = key_vectors.shape[1]
    sharing = queries.shape[1] // key_heads
    blocks = row_total_count // block_row_span
    scaling = HEAD_SIZE ** (-0.5)
    grouped_heads = queries.reshape(blocks, block_row_span, key_heads, sharing, HEAD_SIZE)
    grad_grouped = out_grad.reshape(blocks, block_row_span, key_heads, sharing, HEAD_SIZE)

    def one_block(running, element):
        key_sum, value_sum = running
        query_tile_block, grad_block, log_block, segment_block, place_block = element
        allowed = mask_for(segment_block, place_block, segment, places)
        scores = scores_for(query_tile_block, key_vectors)
        probability = jnp.where(allowed, jnp.exp(scores - log_block), 0.0)
        probability_low = probability.astype(jnp.bfloat16)
        value_sum = value_sum + jnp.einsum(
            "kgqs,qkgd->skd", probability_low, grad_block, preferred_element_type=jnp.float32
        )
        prob_grad = jnp.einsum(
            "qkgd,skd->kgqs", grad_block, value_vectors, preferred_element_type=jnp.float32
        )
        centre = jnp.sum(probability * prob_grad, axis=-1, keepdims=True)
        score_grad = (probability * (prob_grad - centre)).astype(jnp.bfloat16)
        query_grad = (
            jnp.einsum(
                "kgqs,skd->qkgd", score_grad, key_vectors, preferred_element_type=jnp.float32
            )
            * scaling
        )
        key_sum = (
            key_sum
            + jnp.einsum(
                "kgqs,qkgd->skd", score_grad, query_tile_block, preferred_element_type=jnp.float32
            )
            * scaling
        )
        return ((key_sum, value_sum), query_grad.reshape(block_row_span, -1, HEAD_SIZE))

    empty = jnp.zeros(key_vectors.shape, jnp.float32)
    (key_grad, value_grad), query_grads = lax.scan(
        one_block,
        (empty, empty),
        (
            grouped_heads,
            grad_grouped,
            log_totals,
            segment.reshape(blocks, block_row_span),
            places.reshape(blocks, block_row_span),
        ),
    )
    return (query_grads.reshape(row_total_count, -1, HEAD_SIZE), key_grad, value_grad)


def body(
    tokens_own,
    cotangent_own,
    doc_lengths,
    query_weight,
    key_value_weight,
    output_weight,
    gateup_weight,
    down_weight,
    norm_gains,
    query_momentum,
    keyval_momentum,
    output_momentum,
    gateup_momentum,
    down_momentum,
    gains_momentum,
    query_average,
    key_value_mean,
    output_average,
    gateup_average,
    down_average,
    gains_average,
):
    group_rows = 1024
    block_row_span = 512
    rates = step_rates(16384)
    native = lax.axis_index("core") == lax.axis_index("yhi")
    qkv_own = jnp.concatenate(
        [query_weight, key_value_weight[0], key_value_weight[1]], axis=1
    ).astype(BF16)
    lengths = jnp.pad(doc_lengths, ((0, 7), (0, 124)))
    tokens, qkv_piece, output_piece, gains_rows, lengths_there = enter(
        tokens_own,
        qkv_own,
        output_weight.astype(BF16),
        jnp.pad(norm_gains, (0, 94)).reshape(1, 1, 128),
        lengths,
    )
    gains_full = (
        gains_rows.reshape(4, 2, 2, 4, 2, 128)[..., :34].transpose(0, 2, 4, 1, 3, 5).reshape(4352)
    )
    gain_first = gains_full[:MODEL_WIDTH]
    gain_second = gains_full[MODEL_WIDTH : 2 * MODEL_WIDTH]
    gain_query = gains_full[2 * MODEL_WIDTH : 2 * MODEL_WIDTH + HEAD_SIZE]
    key_norm_gain = gains_full[2 * MODEL_WIDTH + HEAD_SIZE :]
    length_row = jnp.where(native, doc_lengths[0], lengths_there[0, :4])
    segment, places, cosine_table, sine_table = doc_layout(length_row, group_rows)
    inputs = tokens.astype(jnp.float32)
    first_normed, first_pull = jax.vjp(root_mean_norm, inputs, gain_first)
    first_low = first_normed.astype(jnp.bfloat16)
    normed_all, qkv_full, output_full, cotangent, gate_piece, up_piece, down_piece = first_gather(
        first_low,
        qkv_piece,
        output_piece,
        cotangent_own,
        gateup_weight[0].astype(BF16),
        gateup_weight[1].astype(BF16),
        down_weight.astype(BF16),
    )
    parts = product(normed_all, qkv_full)
    query_part, key_slice, value_slice = parts[:, :256], parts[:, 256:384], parts[:, 384:]

    def turn_both(query_in, key_in, query_scale, key_scale):
        return (
            head_turn(query_in, query_scale, cosine_table, sine_table),
            head_turn(key_in, key_scale, cosine_table, sine_table),
        )

    (query_turned, key_turned), turn_pull = jax.vjp(
        turn_both, query_part, key_slice, gain_query, key_norm_gain
    )
    queries = query_turned.astype(jnp.bfloat16)
    key_vectors = key_turned.astype(jnp.bfloat16)
    value_vectors = value_slice.astype(jnp.bfloat16).reshape(group_rows, -1, HEAD_SIZE)
    attended, log_totals = attend_forward(
        queries, key_vectors, value_vectors, segment, places, block_row_span
    )
    attended_low = attended.reshape(group_rows, -1).astype(jnp.bfloat16)
    attention_out, gate_full = sum_and_weight(
        2, product(attended_low, output_full).astype(BF16), gate_piece, (2048, 768), gateup_spot
    )
    residual = inputs + attention_out
    second_normed, second_pull = jax.vjp(root_mean_norm, residual, gain_second)
    second_low = second_normed.astype(jnp.bfloat16)
    second_all, up_full = gather_and_weight(3, second_low, up_piece, (2048, 768), gateup_spot)
    upstream_all, down_full = gather_and_weight(4, cotangent, down_piece, (768, 2048), down_spot)
    gate_value = product(second_all, gate_full)
    upward = product(second_all, up_full)
    activated, swiglu_pull = jax.vjp(swiglu, gate_value, upward)
    hidden = activated.astype(jnp.bfloat16)
    mlp_terms = product(hidden, down_full).astype(BF16)
    hidden_grad = contract_last(upstream_all, down_full)
    down_grad = contract_first(hidden, upstream_all).astype(BF16)
    gate_grad, upward_grad = swiglu_pull(hidden_grad)
    gate_low = gate_grad.astype(jnp.bfloat16)
    upward_low = upward_grad.astype(jnp.bfloat16)
    gate_weight_grad = contract_first(second_all, gate_low).astype(BF16)
    up_weight_grad = contract_first(second_all, upward_low).astype(BF16)
    second_terms = (contract_last(gate_low, gate_full) + contract_last(upward_low, up_full)).astype(
        BF16
    )
    second_grad, down_total = sum_and_gradient(5, second_terms, down_grad, (384, 256), down_spot)
    residual_part, second_gain_grad = second_pull(second_grad)
    residual_grad = cotangent.astype(jnp.float32) + residual_part
    residual_low = residual_grad.astype(jnp.bfloat16)
    residual_all, gate_total = gather_and_gradient(
        6, residual_low, gate_weight_grad, (256, 384), gateup_spot
    )
    output_grad = contract_first(attended_low, residual_all).astype(BF16)
    attended_grad = contract_last(residual_all, output_full).astype(jnp.bfloat16)
    query_rot_grad, key_rot_grad, value_grad = attend_backward(
        queries,
        key_vectors,
        value_vectors,
        attended_grad,
        log_totals,
        segment,
        places,
        block_row_span,
    )
    query_part_grad, key_part_grad, query_gain_grad, key_gain_grad = turn_pull(
        (query_rot_grad, key_rot_grad)
    )
    parts_grad = jnp.concatenate(
        [query_part_grad, key_part_grad, value_grad.reshape(group_rows, -1)], axis=1
    ).astype(BF16)
    first_terms = contract_last(parts_grad, qkv_full).astype(BF16)
    first_grad, up_total = sum_and_gradient(
        7, first_terms, up_weight_grad, (256, 384), gateup_spot
    )
    qkv_grad = contract_first(normed_all, parts_grad).astype(BF16)
    input_part, first_gain_grad = first_pull(first_grad)
    input_grad = (residual_grad + input_part).astype(jnp.bfloat16)
    gain_terms = jnp.concatenate(
        [first_gain_grad, second_gain_grad, query_gain_grad, key_gain_grad]
    )
    gain_rows = jnp.pad(
        gain_terms.reshape(4, 2, 2, 2, 4, 34).transpose(0, 3, 1, 4, 2, 5).reshape(128, 1, 34),
        ((0, 0), (0, 0), (0, 94)),
    )
    mlp_out, qkv_total, output_total, gains_total = last_sums(
        mlp_terms, qkv_grad, output_grad, gain_rows
    )
    block_out = (residual + mlp_out).astype(jnp.bfloat16)
    block_out, input_grad, qkv_total, output_total, gate_total, up_total, down_total = leave(
        block_out, input_grad, qkv_total, output_total, gate_total, up_total, down_total
    )
    masters = (
        query_weight,
        key_value_weight,
        output_weight,
        gateup_weight,
        down_weight,
        norm_gains,
    )
    gradients = (
        qkv_total[:, :256].astype(F32),
        jnp.stack([qkv_total[:, 256:384], qkv_total[:, 384:]]).astype(F32),
        output_total.astype(F32),
        jnp.stack([gate_total, up_total]).astype(F32),
        down_total.astype(F32),
        gains_total.reshape(128)[:34],
    )
    moments = (
        query_momentum,
        keyval_momentum,
        output_momentum,
        gateup_momentum,
        down_momentum,
        gains_momentum,
    )
    averages = (
        query_average,
        key_value_mean,
        output_average,
        gateup_average,
        down_average,
        gains_average,
    )
    updated = []
    velocity = []
    smoothed = []
    for master, gradient, moment, average, rate in zip(
        masters, gradients, moments, averages, rates
    ):
        moment_next = MOMENTUM * moment + gradient
        master_next = master - rate * (gradient + MOMENTUM * moment_next)
        updated.append(master_next)
        velocity.append(moment_next)
        smoothed.append(AVERAGING * average + (1.0 - AVERAGING) * master_next)
    return (block_out, input_grad, *updated, *velocity, *smoothed)


def solution(mesh):
    parted = Mesh(mesh.devices.reshape(GRID), AXES)
    data = ("z", "ylo", "core")
    tensor = ("yhi", "x")
    rows = P(AXES, None)
    by_rows = P(data, tensor)
    pair = P(None, data, tensor)
    by_columns = P(tensor, data)
    flat = P(AXES)
    weights = (by_rows, pair, by_columns, pair, by_columns, flat)
    return jax.shard_map(
        body,
        mesh=parted,
        in_specs=(rows, rows, P(data, None)) + weights * 3,
        out_specs=(rows, rows) + weights * 3,
        check_vma=False,
    )
```

time: 986 us -> 494 us (0.50)
  waiting for transfers between devices: 570 us -> 0 us
  Pallas kernels: 0 us -> 279 us
  blocking collectives: 140 us -> 0 us
  local copies, waits for them, and re-layouts: 53.4 us -> 37.2 us
  starting transfers between devices: 16.1 us -> 0 us
  other arithmetic: 66.3 us -> 51.4 us
  between operations: 15.1 us -> 2.32 us
    reduce_scatter x5 -> x0, waiting for transfers between devices: 310 us -> none  [the longest x1 82.1 us: body(): lax.psum_scatter((contract_last(gate_low, gateup_back[0]) + contract_last...]
    pallas_call x0 -> x10, Pallas kernels: none -> 279 us  [__call__(): pl.pallas_call(kernel, out_shape=[shape for shape, _ in outs], in_specs=s...]
    all_gather x5 -> x0, waiting for transfers between devices: 232 us -> none  [the longest x1 71.3 us: body(): portion = lax.all_gather(first_low, 'tensor', axis=0, tiled=True)]
    unnamed x2 -> x0, blocking collectives: 140 us -> none
    all_to_all x3 -> x0, waiting for transfers between devices: 27.1 us -> none  [summed_on_arrival(): lax.all_to_all(tiles, axis, split_axis=0, concat_axis=0, tiled=True)]
    all_to_all x3 -> x0, starting transfers between devices: 15.3 us -> none  [summed_on_arrival(): lax.all_to_all(tiles, axis, split_axis=0, concat_axis=0, tiled=True)]
    dot_general x7 -> x5, matrix products: 31.3 us -> 19.1 us  [contract_first(): lax.dot_general(left, right, (((0,), (0,)), ((), ())), preferred_element_...]
    dot_general x7 -> x5, matrix products: 36.9 us -> 28.5 us  [product(): return jnp.dot(left, right, preferred_element_type=jnp.float32)]
  transfers between devices with their start and end apart: 14 -> 0, of which waited for: 12 -> 0; matrix products, arithmetic and copies ran while one was open for 16% -> 0% of each run, Pallas kernels for 0% -> 0%
where the time goes in v1:
time: 494 us; the launch traced here: 484 us
  Pallas kernels  279 us (56%)
  matrix products  113 us (23%)
  other arithmetic  51.4 us (10%)
  local copies, waits for them, and re-layouts  37.2 us (8%)
    pallas_call x10, Pallas kernels, __call__(): pl.pallas_call(kernel, out_shape=[shape for shape, _ in outs], in_specs=s...  279 us
    dot_general x5, matrix products, contract_last(): lax.dot_general(left, right, (((1,), (1,)), ((), ())), preferred_element_...  31.5 us
    dot_general x5, matrix products, product(): return jnp.dot(left, right, preferred_element_type=jnp.float32)  28.5 us
    dot_general x5, matrix products, contract_first(): lax.dot_general(left, right, (((0,), (0,)), ((), ())), preferred_element_...  19.1 us
    cos x2, other arithmetic, doc_layout(): return (segment, places, jnp.cos(angles), jnp.sin(angles))  12.7 us
    unnamed x168, local copies, waits for them, and re-layouts  11.3 us

profile of v1, /device:TPU:1, one launch (start us, length us, event | category | flops | bytes accessed | tf_op | source)
XLA Modules:
  0.0 483.8 jit_solution(9614677637102246103)
XLA Ops:
  5.9 19.1 %links_0.1 = (bf16[128,2048]{1,0:T(8,128)(2,1)S(1)}, bf16[128,512]{1,0:T(8,128)(2,1)S(1)}, bf16[256,128]{1,0:T(8,128)(2,1)S(1)}, f32[128,1,128]{2,1,0:T(1,128)S(1)}, s32[8,128]{1,0:T(8,128)S(1)}) custom-call(bf16[128,2048]{1,0:T(8,128)(2,1)S(1)} %copy-done.2, bf16[128,512]{1,0:T(8,128)(2,1)S(1)} %pad_maximum_fusion.7.refs_1_, ...), custom_call_target="tpu_custom_call" | custom-call | tf_op jit(solution)/shard_map/links_0/pallas_call | solution.py:512
  27.4 33.4 %links_1.1 = (bf16[1024,2048]{1,0:T(8,128)(2,1)}, bf16[2048,512]{1,0:T(8,128)(2,1)S(1)}, bf16[256,2048]{1,0:T(8,128)(2,1)S(1)}, bf16[128,2048]{1,0:T(8,128)(2,1)...) custom-call(bf16[128,2048]{1,0:T(8,128)(2,1)S(1)} %fusion.59.refs_0_, ...), custom_call_target="tpu_custom_call" | custom-call | tf_op jit(solution)/shard_map/links_1/pallas_call | solution.py:512
  60.8 5.3 %fusion.121 = f32[1024,512]{0,1:T(8,128)S(1)} fusion(bf16[1024,2048]{1,0:T(8,128)(2,1)} %get-tuple-element.182, bf16[2048,512]{1,0:T(8,128)(2,1)S(1)} %get-tuple-element.183), kind=kOutput, calls=%fused_computation.225 | convolution fusion | flops 2147483648 | bytes 8388608 | tf_op jit(solution)/shard_map/dot_general | solution.py:851
  69.5 4.4 fusion.73
  83.9 3.1 reshape.571
  87.2 8.4 %fusion.87 = (f32[2,512,128]{1,0,2:T(2,128)S(1)}, f32[2,512,128]{1,0,2:T(2,128)S(1)}) fusion(f32[2,512,64]{1,0,2:T(2,128)S(1)} %broadcast_multiply_fusion.2), kind=kLoop, calls=%fused_computation.153 | loop fusion | flops 131072 | bytes 1310720 | tf_op jit(solution)/shard_map/cos | solution.py:823
  95.6 4.0 fusion.68
  103.4 14.8 %while.28 = (s32[]{:T(128)}, bf16[2,512,256]{2,1,0:T(8,128)(2,1)}, f32[2,1,2,512,1]{3,2,4,1,0:T(2,128)S(1)}, s32[2,512]{1,0:T(2,128)S(1)}, s32[1024]{0:T(1024)S(...) while((s32[]{:T(128)}, bf16[2,512,256]{2,1,0:T(8,128)(2,1)}, ...), condition=%wide.region_9.10_spmd.clone, body=%wide.region_6.9_spmd.clone.sunk | while | flops 551025664 | bytes 16827500 | solution.py:896
  118.2 4.4 convolution_convert_fusion.1.refs_0_
  122.7 33.2 %links_2.1 = (f32[128,2048]{1,0:T(8,128)S(1)}, bf16[2048,768]{1,0:T(8,128)(2,1)S(1)}) custom-call(bf16[1024,2048]{1,0:T(8,128)(2,1)} %convolution_convert_fusion.1.refs_0_, bf16[256,384]{1,0:T(8,128)(2,1)S(1)} %get-tuple-element.186.refs_1_), custom_call_target="tpu_custom_call" | custom-call | tf_op jit(solution)/shard_map/links_2/pallas_call | solution.py:512
  157.0 26.9 %links_3.1 = (bf16[1024,2048]{1,0:T(8,128)(2,1)}, bf16[2048,768]{1,0:T(8,128)(2,1)S(1)}) custom-call(bf16[128,2048]{1,0:T(8,128)(2,1)S(1)} %multiply_convert_fusion.2.refs_0_, bf16[256,384]{1,0:T(8,128)(2,1)S(1)} %get-tuple-element.188.refs_1_), custom_call_target="tpu_custom_call" | custom-call | tf_op jit(solution)/shard_map/links_3/pallas_call | solution.py:512
  184.0 8.4 %fusion.123 = f32[1024,768]{1,0:T(8,128)} fusion(bf16[1024,2048]{1,0:T(8,128)(2,1)} %get-tuple-element.189, bf16[2048,768]{1,0:T(8,128)(2,1)S(1)} %get-tuple-element.191), kind=kOutput, calls=%fused_computation.227 | convolution fusion | flops 3221225472 | bytes 10485760 | tf_op jit(solution)/shard_map/dot_general | solution.py:851
  192.4 5.1 %fusion.122 = f32[1024,768]{1,0:T(8,128)} fusion(bf16[1024,2048]{1,0:T(8,128)(2,1)S(1)} %copy-done.84, bf16[2048,768]{1,0:T(8,128)(2,1)S(1)} %get-tuple-element.190), kind=kOutput, calls=%fused_computation.226 | convolution fusion | flops 3221225472 | bytes 10485760 | tf_op jit(solution)/shard_map/dot_general | solution.py:851
  197.5 27.9 %links_4.1 = (bf16[1024,2048]{1,0:T(8,128)(2,1)}, bf16[768,2048]{1,0:T(8,128)(2,1)S(1)}) custom-call(bf16[128,2048]{1,0:T(8,128)(2,1)S(1)} %get-tuple-element.192.refs_0_, bf16[384,256]{1,0:T(8,128)(2,1)S(1)} %get-tuple-element.193.refs_1_), custom_call_target="tpu_custom_call" | custom-call | tf_op jit(solution)/shard_map/links_4/pallas_call | solution.py:512
  225.5 9.6 %multiply_convert_fusion = (bf16[1024,768]{1,0:T(8,128)(2,1)S(1)}, bf16[1024,768]{1,0:T(8,128)(2,1)S(1)}, bf16[1024,768]{1,0:T(8,128)(2,1)S(1)}) fusion(f32[1024,768]{1,0:T(8,128)} %fusion.122, f32[1024,768]{1,0:T(8,128)} %fusion.123, bf16[1024,2048]{1,0:T(8,128)(2,1)} %get-tuple-element.196, bf16[768,2048]{1,0:T(8,128)(2,1)S(1)} %get-tuple-element.194), kind=kOutput, calls=%fused_computation.76 | convolution fusion | flops 3233808384 | bytes 18350080 | tf_op jit(solution)/shard_map/dot_general | solution.py:855
  235.1 5.4 %convolution_convert_fusion.3.refs_1_ = bf16[2048,768]{1,0:T(8,128)(2,1)} fusion(bf16[1024,2048]{1,0:T(8,128)(2,1)S(1)} %copy-done.84, bf16[1024,768]{1,0:T(8,128)(2,1)S(1)} %get-tuple-element.465), kind=kOutput, calls=%fused_computation.70 | convolution fusion | flops 3222798336 | bytes 8912896 | tf_op jit(solution)/shard_map/dot_general | solution.py:861
  240.5 3.7 convolution_convert_fusion.4.refs_1_
  244.2 3.7 convolution_convert_fusion.5.refs_1_
  247.9 5.8 %fusion.124 = f32[1024,2048]{1,0:T(8,128)} fusion(bf16[1024,768]{1,0:T(8,128)(2,1)S(1)} %get-tuple-element.466, bf16[2048,768]{1,0:T(8,128)(2,1)S(1)} %get-tuple-element.190), kind=kOutput, calls=%fused_computation.228 | convolution fusion | flops 3221225472 | bytes 13107200 | tf_op jit(solution)/shard_map/dot_general | solution.py:855
  253.7 7.4 %add_convert_fusion.refs_0_ = bf16[1024,2048]{1,0:T(8,128)(2,1)} fusion(f32[1024,2048]{1,0:T(8,128)} %fusion.124, bf16[1024,768]{1,0:T(8,128)(2,1)S(1)} %get-tuple-element.465, bf16[2048,768]{1,0:T(8,128)(2,1)S(1)} %copy-done.8), kind=kOutput, calls=%fused_computation.65 | convolution fusion | flops 3225419776 | bytes 17301504 | tf_op jit(solution)/shard_map/dot_general | solution.py:855
  261.2 30.2 %links_5.1 = (f32[128,2048]{1,0:T(8,128)S(1)}, bf16[384,256]{1,0:T(8,128)(2,1)S(1)}) custom-call(bf16[1024,2048]{1,0:T(8,128)(2,1)} %add_convert_fusion.refs_0_, bf16[768,2048]{1,0:T(8,128)(2,1)S(1)} %convolution_convert_fusion.5.refs_1_), custom_call_target="tpu_custom_call" | custom-call | tf_op jit(solution)/shard_map/links_5/pallas_call | solution.py:512
  293.2 25.0 %links_6.1 = (bf16[1024,2048]{1,0:T(8,128)(2,1)}, bf16[256,384]{1,0:T(8,128)(2,1)S(1)}) custom-call(bf16[128,2048]{1,0:T(8,128)(2,1)S(1)} %fusion.109.refs_0_, bf16[2048,768]{1,0:T(8,128)(2,1)S(1)} %convolution_convert_fusion.4.refs_1_), custom_call_target="tpu_custom_call" | custom-call | tf_op jit(solution)/shard_map/links_6/pallas_call | solution.py:512
  318.2 4.3 convolution_convert_fusion.8
  325.6 34.1 %while.29 = (s32[]{:T(128)}, f32[1024,1,128]{0,2,1:T(8,128)}, f32[1024,1,128]{0,2,1:T(8,128)}, f32[2,512,2,128]{3,1,0,2:T(8,128)}, bf16[2,512,1,2,128]{4,1,3,2,0...) while((s32[]{:T(128)}, f32[1024,1,128]{0,2,1:T(8,128)}, ...), condition=%wide.region_14.15_spmd.clone, body=%wide.region_12.14_spmd.clone.sunk | while | flops 1360264192 | bytes 69023584 | solution.py:948
  338.1 4.3 fusion.193
  355.0 4.5 fusion.193
  371.0 4.4 convolution_convert_fusion.refs_0_
  375.5 33.4 %links_7.1 = (f32[128,2048]{1,0:T(8,128)S(1)}, bf16[256,384]{1,0:T(8,128)(2,1)S(1)}) custom-call(bf16[1024,2048]{1,0:T(8,128)(2,1)} %convolution_convert_fusion.refs_0_, bf16[2048,768]{1,0:T(8,128)(2,1)S(1)} %copy-done), custom_call_target="tpu_custom_call" | custom-call | tf_op jit(solution)/shard_map/links_7/pallas_call | solution.py:512
  413.6 3.8 convolution_convert_fusion.7.refs_2_
  420.0 5.3 %convolution_convert_fusion.2.refs_0_ = bf16[1024,2048]{1,0:T(8,128)(2,1)} fusion(bf16[1024,768]{1,0:T(8,128)(2,1)S(1)} %copy-done.87, bf16[768,2048]{1,0:T(8,128)(2,1)S(1)} %copy-done.6), kind=kOutput, calls=%fused_computation.69 | convolution fusion | flops 3223322624 | bytes 8912896 | tf_op jit(solution)/shard_map/dot_general | solution.py:851
  425.3 31.6 %links_8.1 = (f32[128,2048]{1,0:T(8,128)S(1)}, bf16[128,512]{1,0:T(8,128)(2,1)S(1)}, bf16[256,128]{1,0:T(8,128)(2,1)S(1)}, f32[1,1,128]{2,1,0:T(1,128)S(1)}) custom-call(bf16[1024,2048]{1,0:T(8,128)(2,1)} %convolution_convert_fusion.2.refs_0_, bf16[2048,512]{1,0:T(8,128)(2,1)S(1)} %convolution_convert_fusion.6.refs_1_, ...), custom_call_target="tpu_custom_call" | custom-call | tf_op jit(solution)/shard_map/links_8/pallas_call | solution.py:512
  457.9 18.1 %links_9.1 = (bf16[128,2048]{1,0:T(8,128)(2,1)S(1)}, bf16[128,2048]{1,0:T(8,128)(2,1)S(1)}, bf16[128,512]{1,0:T(8,128)(2,1)S(1)}, bf16[256,128]{1,0:T(8,128)(2,1...) custom-call(bf16[128,2048]{1,0:T(8,128)(2,1)S(1)} %get-tuple-element.469.refs_0_, ...), custom_call_target="tpu_custom_call" | custom-call | tf_op jit(solution)/shard_map/links_9/pallas_call | solution.py:512
  (308 shorter events, 96.7 us)
Async XLA Ops:
  0.7 26.6 %copy-start.29 = (f32[768,128]{1,0:T(8,128)S(1)}, f32[768,128]{1,0:T(8,128)}, u32[]{:S(2)}) copy-start(f32[768,128]{1,0:T(8,128)} %param.32) | copy-start | bytes 1179652
  0.7 26.7 %copy-start.1 = (bf16[128,2048]{1,0:T(8,128)(2,1)S(1)}, bf16[128,2048]{1,0:T(8,128)(2,1)}, u32[]{:S(2)}) copy-start(bf16[128,2048]{1,0:T(8,128)(2,1)} %refs_3_.1) | copy-start | bytes 1572868
  25.2 35.6 %copy-start.71 = (f32[128]{0:T(128)}, f32[128]{0:T(128)S(1)}, u32[]{:S(2)}) copy-start(f32[128]{0:T(128)S(1)} %fusion.103) | copy-start | bytes 1540
  25.9 40.3 %copy-start.48 = (f32[2048]{0:T(1024)}, f32[2048]{0:T(1024)S(1)}, u32[]{:S(2)}) copy-start(f32[2048]{0:T(1024)S(1)} %get-tuple-element.490) | copy-start | bytes 24580
  60.8 7.5 %copy-start.76 = (s32[1,4]{1,0:T(1,128)S(1)}, s32[1,4]{1,0:T(1,128)}, u32[]{:S(2)}) copy-start(s32[1,4]{1,0:T(1,128)} %param.27) | copy-start | bytes 52
  66.3 7.7 %copy-start.56 = (f32[1024]{0:T(1024)}, f32[1024]{0:T(1024)S(1)}, u32[]{:S(2)}) copy-start(f32[1024]{0:T(1024)S(1)} %fusion.100) | copy-start | bytes 12292
  66.3 7.5 %copy-start.65 = (f32[128]{0:T(128)}, f32[128]{0:T(128)S(1)}, u32[]{:S(2)}) copy-start(f32[128]{0:T(128)S(1)} %get-tuple-element.491) | copy-start | bytes 1540
  66.3 29.3 %copy-start.67 = (f32[128]{0:T(128)}, f32[128]{0:T(128)S(1)}, u32[]{:S(2)}) copy-start(f32[128]{0:T(128)S(1)} %get-tuple-element.492) | copy-start | bytes 1540
  75.3 6.3 %copy-start.58 = (f32[1024,2]{0,1:T(2,128)}, f32[1024,2]{0,1:T(2,128)S(1)}, u32[]{:S(2)}) copy-start(f32[1024,2]{0,1:T(2,128)S(1)} %multiply_reduce_fusion.5) | copy-start | bytes 24580
  75.4 6.2 %copy-start.44 = (f32[1024,2]{0,1:T(2,128)}, f32[1024,2]{0,1:T(2,128)S(1)}, u32[]{:S(2)}) copy-start(f32[1024,2]{0,1:T(2,128)S(1)} %fusion.99) | copy-start | bytes 24580
  156.1 136.2 %copy-start.69 = (f32[128]{0:T(128)}, f32[128]{0:T(128)S(1)}, u32[]{:S(2)}) copy-start(f32[128]{0:T(128)S(1)} %fusion.104) | copy-start | bytes 1540
  184.0 8.4 %copy-start.7 = (bf16[2048,768]{1,0:T(8,128)(2,1)}, bf16[2048,768]{1,0:T(8,128)(2,1)S(1)}, u32[]{:S(2)}) copy-start(bf16[2048,768]{1,0:T(8,128)(2,1)S(1)} %get-tuple-element.191) | copy-start | bytes 9437188
  184.0 8.4 %copy-start.84 = (bf16[1024,2048]{1,0:T(8,128)(2,1)S(1)}, bf16[1024,2048]{1,0:T(8,128)(2,1)}, u32[]{:S(2)}) copy-start(bf16[1024,2048]{1,0:T(8,128)(2,1)} %get-tuple-element.189) | copy-start | bytes 12582916
  225.4 9.6 %copy-start.5 = (bf16[768,2048]{1,0:T(8,128)(2,1)}, bf16[768,2048]{1,0:T(8,128)(2,1)S(1)}, u32[]{:S(2)}) copy-start(bf16[768,2048]{1,0:T(8,128)(2,1)S(1)} %get-tuple-element.194) | copy-start | bytes 9437188
  235.1 9.1 %copy-start.86 = (bf16[1024,768]{1,0:T(8,128)(2,1)}, bf16[1024,768]{1,0:T(8,128)(2,1)S(1)}, u32[]{:S(2)}) copy-start(bf16[1024,768]{1,0:T(8,128)(2,1)S(1)} %get-tuple-element.467) | copy-start | bytes 4718596
  247.9 5.8 %copy-start.8 = (bf16[2048,768]{1,0:T(8,128)(2,1)S(1)}, bf16[2048,768]{1,0:T(8,128)(2,1)}, u32[]{:S(2)}) copy-start(bf16[2048,768]{1,0:T(8,128)(2,1)} %copy-done.7) | copy-start | bytes 9437188
  261.2 30.2 %copy-start.18 = (f32[128,2048]{1,0:T(8,128)S(1)}, f32[128,2048]{1,0:T(8,128)}, u32[]{:S(2)}) copy-start(f32[128,2048]{1,0:T(8,128)} %copy-done.17) | copy-start | bytes 3145732
  375.5 34.1 %copy-start.49 = (f32[2048]{0:T(1024)S(1)}, f32[2048]{0:T(1024)}, u32[]{:S(2)}) copy-start(f32[2048]{0:T(1024)} %copy-done.48) | copy-start | bytes 24580
  375.5 34.1 %copy-start.72 = (f32[128]{0:T(128)S(1)}, f32[128]{0:T(128)}, u32[]{:S(2)}) copy-start(f32[128]{0:T(128)} %copy-done.71) | copy-start | bytes 1540
  375.5 35.0 %copy-start.64 = (f32[2048]{0:T(1024)S(1)}, f32[2048]{0:T(1024)}, u32[]{:S(2)}) copy-start(f32[2048]{0:T(1024)} %get-tuple-element.385) | copy-start | bytes 24580
  425.3 31.7 %copy-start.78 = (f32[128]{0:T(128)S(1)}, f32[128]{0:T(128)}, u32[]{:S(2)}) copy-start(f32[128]{0:T(128)} %copy-done.77) | copy-start | bytes 1540
  425.3 31.7 %copy-start.79 = (f32[128]{0:T(128)S(1)}, f32[128]{0:T(128)}, u32[]{:S(2)}) copy-start(f32[128]{0:T(128)} %get-tuple-element.387) | copy-start | bytes 1540
  425.3 31.7 %copy-start.19 = (f32[128,2048]{1,0:T(8,128)S(1)}, f32[128,2048]{1,0:T(8,128)}, u32[]{:S(2)}) copy-start(f32[128,2048]{1,0:T(8,128)} %copy-done.17) | copy-start | bytes 3145732
  425.3 31.7 %copy-start.70 = (f32[128]{0:T(128)S(1)}, f32[128]{0:T(128)}, u32[]{:S(2)}) copy-start(f32[128]{0:T(128)} %copy-done.69) | copy-start | bytes 1540
  425.3 31.7 %copy-start.73 = (f32[128]{0:T(128)S(1)}, f32[128]{0:T(128)}, u32[]{:S(2)}) copy-start(f32[128]{0:T(128)} %copy-done.71) | copy-start | bytes 1540
  425.3 31.7 %copy-start.75 = (f32[128]{0:T(128)S(1)}, f32[128]{0:T(128)}, u32[]{:S(2)}) copy-start(f32[128]{0:T(128)} %copy-done.74) | copy-start | bytes 1540
  457.0 19.1 %copy-start.26 = (f32[2,128,768]{2,1,0:T(8,128)S(1)}, f32[2,128,768]{2,1,0:T(8,128)}, u32[]{:S(2)}) copy-start(f32[2,128,768]{2,1,0:T(8,128)} %param.31) | copy-start | bytes 2359300
  457.0 19.1 %copy-start.31 = (f32[2,128,768]{2,1,0:T(8,128)S(1)}, f32[2,128,768]{2,1,0:T(8,128)}, u32[]{:S(2)}) copy-start(f32[2,128,768]{2,1,0:T(8,128)} %param.43) | copy-start | bytes 2359300
  457.0 19.1 %copy-start.32 = (f32[2,128,768]{2,1,0:T(8,128)S(1)}, f32[2,128,768]{2,1,0:T(8,128)}, u32[]{:S(2)}) copy-start(f32[2,128,768]{2,1,0:T(8,128)} %param.37) | copy-start | bytes 2359300
  457.9 19.9 %copy-start.33 = (f32[2,128,128]{2,1,0:T(8,128)S(1)}, f32[2,128,128]{2,1,0:T(8,128)}, u32[]{:S(2)}) copy-start(f32[2,128,128]{2,1,0:T(8,128)} %param.29) | copy-start | bytes 393220
  457.9 19.9 %copy-start.50 = (f32[2,128,128]{2,1,0:T(8,128)S(1)}, f32[2,128,128]{2,1,0:T(8,128)}, u32[]{:S(2)}) copy-start(f32[2,128,128]{2,1,0:T(8,128)} %param.41) | copy-start | bytes 393220
  457.9 19.9 %copy-start.51 = (f32[2,128,128]{2,1,0:T(8,128)S(1)}, f32[2,128,128]{2,1,0:T(8,128)}, u32[]{:S(2)}) copy-start(f32[2,128,128]{2,1,0:T(8,128)} %param.35) | copy-start | bytes 393220
  (63 other events, 190.9 us)
